TPU v7x, 128 devices: a whole 4x4x4 slice. The times are simulated.
128 devices in a mesh: stream: 16 (over z, y), span: 2 (over core), vert: 4 (over x).
Axes of the slice: x: 4, y: 4, z: 4, core: 2. Of those that a mesh axis runs over, the one named last changes fastest.
Arguments:
- velocity: float32 [3, 48, 32, 32, 2048], P(None, None, 'vert', 'span', 'stream'), may hold values from -60 to 60, as said below
Outputs:
- modes: float32 [3, 48, 32, 32, 2048], P(None, None, 'vert', 'span', 'stream')
- factor: float32 [48, 48], replicated
Inputs may be any that keep to these rules, and one draw needn't show every extreme that they name: Finite velocity components.
All inputs are finite; a program needn't handle non-finite values.
Results may differ from a plain program's by a relative error of at most 0.0003.
Values sent between devices are 32-bit elements; how exact they have to be, the bound alone decides.
No kernel may reach another device: no remote copies, remote signals or barrier semaphores. Data moves between devices by JAX's collectives and lax.ppermute only.
A program may use at most 192 MiB of HBM per device.

v0:
```python
import functools

import jax
import jax.numpy as jnp
from jax import lax
from jax.experimental import pallas as pl
from jax.experimental.pallas import tpu as pltpu
from jax.sharding import PartitionSpec as P

F32, BF16 = jnp.float32, jnp.bfloat16
HIGH = lax.Precision.HIGHEST
S, NZ, NY, NX = 48, 8, 16, 128
ROWS = NZ * NY
SUB = 8
R = S * SUB
PAIR = 2 * NX
INTERIOR = 20 * PAIR
COLS = 24 * PAIR
MIB = 1 << 20
ALL = ("stream", "span", "vert")
NT = (((1,), (1,)), ((), ()))


def slot(c, z):
    if c == 2:
        return 12 + z
    return c * 6 + z - 1 if 0 < z < NZ - 1 else 20 + 2 * c + (z == NZ - 1)


def any_spec():
    return pl.BlockSpec(memory_space=pl.ANY)


def vmem_spec():
    return pl.BlockSpec(memory_space=pltpu.VMEM)


def params(limit):
    return pltpu.CompilerParams(vmem_limit_bytes=limit * MIB)


def in_vmem(*arrays):
    return [pltpu.with_memory_space_constraint(a, pltpu.VMEM) for a in arrays]


def vertical_faces_kernel(v_ref, head_ref, tail_ref, sems):
    low = pltpu.make_async_copy(v_ref.at[0:2, :, pl.ds(0, NY)], head_ref, sems.at[0])
    high = pltpu.make_async_copy(v_ref.at[0:2, :, pl.ds(ROWS - NY, NY)], tail_ref, sems.at[1])
    low.start()
    high.start()
    low.wait()
    high.wait()


def vertical_faces(v):
    face = pltpu.VMEM((2, S, NY, NX), F32)
    return pl.pallas_call(
        vertical_faces_kernel,
        name="vertical_faces",
        out_shape=(face, face),
        in_specs=[any_spec()],
        out_specs=(vmem_spec(), vmem_spec()),
        scratch_shapes=[pltpu.SemaphoreType.DMA((2,))],
        compiler_params=params(8),
    )(v)


def side_faces_kernel(v_ref, block_ref, x_ref, y_ref, sems):
    copies = [pltpu.make_async_copy(v_ref.at[c], block_ref.at[c], sems.at[c]) for c in range(3)]
    for c in (1, 2, 0):
        copies[c].start()
    lane = lax.broadcasted_iota(jnp.int32, (NY, NX), 1) // 2
    for c in (1, 2):
        copies[c].wait()

        def pack(z, carry, c=c):
            rows = pl.ds(pl.multiple_of(z * NY, NY), NY)
            packed = jnp.zeros((NY, NX), F32)
            for s in range(S):
                turned = pltpu.roll(block_ref[c, s, rows, :], 2 * s + 1, axis=1)
                packed = jnp.where(lane == s, turned, packed)
            x_ref[c - 1, rows, :] = packed
            return carry

        lax.fori_loop(0, NZ, pack, 0)
    copies[0].wait()
    first = lax.axis_index("span") == 0
    for k, c in enumerate((0, 2)):
        for s in range(S):
            high = block_ref[c, s, pl.ds(NY - 1, NZ, stride=NY), :]
            low = block_ref[c, s, pl.ds(0, NZ, stride=NY), :]
            y_ref[k, s] = jnp.where(first, high, low)


def side_faces(v):
    return pl.pallas_call(
        side_faces_kernel,
        name="side_faces",
        out_shape=(
            pltpu.VMEM((3, S, ROWS, NX), F32),
            pltpu.VMEM((2, ROWS, NX), F32),
            pltpu.VMEM((2, S, NZ, NX), F32),
        ),
        in_specs=[any_spec()],
        out_specs=(vmem_spec(), vmem_spec(), vmem_spec()),
        scratch_shapes=[pltpu.SemaphoreType.DMA((3,))],
        compiler_params=params(16),
    )(v)


def split_store(first, second, pair, columns, h_ref, l_ref):
    for half in range(2):
        rows = slice(half * SUB, (half + 1) * SUB)
        value = jnp.concatenate([first[rows], second[rows]], axis=0)
        high = value.astype(BF16)
        low = ((value - high.astype(F32)) * 2.0).astype(BF16)
        where = (pl.ds(pair * 2 * SUB, 2 * SUB), pl.ds(pl.multiple_of(columns + half * NX, NX), NX))
        h_ref[where] = high
        l_ref[where] = low


def interior_kernel(v_ref, hy_ref, left_ref, right_ref, h_ref, l_ref, part_ref, acc_ref, edge_ref):
    row = lax.broadcasted_iota(jnp.int32, (NY, NX), 0)
    lane = lax.broadcasted_iota(jnp.int32, (NY, NX), 1)
    span, stream = lax.axis_index("span"), lax.axis_index("stream")
    first = span == 0
    for c in range(2):
        for z in range(NZ):
            rows = pl.ds(z * NY, NY)
            before = jnp.where(stream > 0, left_ref[c, rows, :], 0.0)
            behind = jnp.where(stream < lax.axis_size("stream") - 1, right_ref[c, rows, :], 0.0)
            edge_ref[c, rows, :] = jnp.where(lane % 2 == 0, before, pltpu.roll(behind, NX - 2, axis=1))

    def at(z):
        return pl.ds(pl.multiple_of(z * NY, NY), NY)

    def dy(c, s, z):
        cells = v_ref[c, s, at(z), :]
        face = hy_ref[c // 2, s, pl.ds(z, 1), :]
        up = jnp.where(row == NY - 1, jnp.where(first, face, 0.0), pltpu.roll(cells, NY - 1, axis=0))
        down = jnp.where(row == 0, jnp.where(first, 0.0, face), pltpu.roll(cells, 1, axis=0))
        return up - down

    def dx(c, s, z):
        cells = v_ref[c, s, at(z), :]
        edge = edge_ref[c - 1, at(z), :]
        if s:
            edge = pltpu.roll(edge, NX - 2 * s, axis=1)
        up = jnp.where(lane == NX - 1, edge, pltpu.roll(cells, NX - 1, axis=1))
        down = jnp.where(lane == 0, edge, pltpu.roll(cells, 1, axis=1))
        return up - down

    def dz(c, s, z):
        return v_ref[c, s, at(z + 1), :] - v_ref[c, s, at(z - 1), :]

    def inner(z, carry):
        for s in range(0, S, 2):
            split_store(
                *(0.5 * (dy(2, t, z) - dz(1, t, z)) for t in (s, s + 1)),
                s // 2, (z - 1) * PAIR, h_ref, l_ref,
            )
            split_store(
                *(0.5 * (dz(0, t, z) - dx(2, t, z)) for t in (s, s + 1)),
                s // 2, (z + 5) * PAIR, h_ref, l_ref,
            )
        return carry

    def level(z, carry):
        for s in range(0, S, 2):
            split_store(
                *(0.5 * (dx(1, t, z) - dy(0, t, z)) for t in (s, s + 1)),
                s // 2, (z + 12) * PAIR, h_ref, l_ref,
            )
        return carry

    def outer(k, carry):
        z = k * (NZ - 1)
        for s in range(S):
            part_ref[0, k, s] = dy(2, s, z)
            part_ref[1, k, s] = dx(2, s, z)
        return carry

    lax.fori_loop(1, NZ - 1, inner, 0)
    lax.fori_loop(0, NZ, level, 0)
    lax.fori_loop(0, 2, outer, 0)

    acc_ref[...] = jnp.zeros_like(acc_ref)
    step = 4 * PAIR

    def products(k, carry):
        columns = pl.ds(pl.multiple_of(k * step, step), step)
        high = h_ref[:, columns]
        acc_ref[...] += lax.dot_general(high, high, NT, preferred_element_type=F32) + lax.dot_general(
            high, l_ref[:, columns], NT, preferred_element_type=F32
        )
        return carry

    lax.fori_loop(0, INTERIOR // step, products, 0)


def interior(block, hy, left, right):
    return pl.pallas_call(
        interior_kernel,
        name="interior",
        out_shape=(
            pltpu.VMEM((R, COLS), BF16),
            pltpu.VMEM((R, COLS), BF16),
            pltpu.VMEM((2, 2, S, NY, NX), F32),
            pltpu.VMEM((R, R), F32),
        ),
        in_specs=[vmem_spec()] * 4,
        out_specs=(vmem_spec(),) * 4,
        scratch_shapes=[pltpu.VMEM((2, ROWS, NX), F32)],
        compiler_params=params(16),
        cost_estimate=pl.CostEstimate(flops=4 * R * R * INTERIOR, bytes_accessed=30 * MIB, transcendentals=0),
    )(*in_vmem(block, hy, left, right))


def lane_fold():
    shape = (R, NX)
    same = lax.broadcasted_iota(jnp.int32, shape, 0) // SUB == lax.broadcasted_iota(jnp.int32, shape, 1)
    return jnp.where(same, 1.0, 0.0)


def same_cell():
    return lax.broadcasted_iota(jnp.int32, (R, R), 0) % SUB == lax.broadcasted_iota(jnp.int32, (R, R), 1) % SUB


def boundary_kernel(v_ref, part_ref, below_ref, above_ref, acc_ref, hi_ref, li_ref, h_ref, l_ref, gram_ref):
    del hi_ref, li_ref
    vert = lax.axis_index("vert")
    has_below, has_above = vert > 0, vert < lax.axis_size("vert") - 1

    def dz(c, s, k):
        if k:
            return jnp.where(has_above, above_ref[c, s], 0.0) - v_ref[c, s, pl.ds((NZ - 2) * NY, NY), :]
        return v_ref[c, s, pl.ds(NY, NY), :] - jnp.where(has_below, below_ref[c, s], 0.0)

    for k in range(2):
        for s in range(0, S, 2):
            split_store(
                *(0.5 * (part_ref[0, k, t] - dz(1, t, k)) for t in (s, s + 1)),
                s // 2, (20 + k) * PAIR, h_ref, l_ref,
            )
            split_store(
                *(0.5 * (dz(0, t, k) - part_ref[1, k, t]) for t in (s, s + 1)),
                s // 2, (22 + k) * PAIR, h_ref, l_ref,
            )
    columns = pl.ds(INTERIOR, COLS - INTERIOR)
    high = h_ref[:, columns]
    total = (
        acc_ref[...]
        + lax.dot_general(high, high, NT, preferred_element_type=F32)
        + lax.dot_general(high, l_ref[:, columns], NT, preferred_element_type=F32)
    )
    total = jnp.where(same_cell(), total, 0.0).reshape(S, SUB, R).sum(1)
    gram_ref[...] = lax.dot_general(
        total, lane_fold(), (((1,), (0,)), ((), ())), precision=HIGH, preferred_element_type=F32
    )


def boundary(block, part, below, above, acc, high, low):
    return pl.pallas_call(
        boundary_kernel,
        name="boundary",
        out_shape=(
            pltpu.VMEM((R, COLS), BF16),
            pltpu.VMEM((R, COLS), BF16),
            pltpu.VMEM((S, NX), F32),
        ),
        in_specs=[vmem_spec()] * 5 + [any_spec()] * 2,
        out_specs=(vmem_spec(),) * 3,
        input_output_aliases={5: 0, 6: 1},
        compiler_params=params(16),
    )(*in_vmem(block, part, below, above, acc, high, low))


def modes_kernel(count, gram_ref, h_ref, l_ref, out_ref, factor_ref, wh_ref, wl_ref):
    @pl.when((pl.program_id(0) == 0) & (pl.program_id(1) == 0))
    def _():
        shape = (S, NX)
        row = lax.broadcasted_iota(jnp.int32, shape, 0)
        lane = lax.broadcasted_iota(jnp.int32, shape, 1)
        raw = gram_ref[...] / count
        square = jnp.concatenate([raw, jnp.zeros((NX - S, NX), F32)], axis=0)
        work = 0.5 * (raw + square.T[:S]) + jnp.where(lane == row + NX // 2, 1.0, 0.0)
        for k in range(S - 1):
            pivot = work[k : k + 1, :]
            scaled = pivot / pivot[:, k : k + 1]
            work = work - jnp.where(row > k, work[:, k : k + 1], 0.0) * scaled
        diagonal = jnp.sum(jnp.where(lane == row, work, 0.0), axis=1, keepdims=True)
        work = work * lax.rsqrt(diagonal)
        factor_ref[...] = jnp.where(lane >= row, work, 0.0)[:, :S]
        inverse = jnp.where(lane <= row, pltpu.roll(work, NX // 2, axis=1), 0.0)
        high = inverse.astype(BF16).astype(F32)
        both = jnp.concatenate([high, inverse - high], axis=0).astype(BF16)
        wide = lax.dot_general(both, lane_fold().astype(BF16), NT, preferred_element_type=F32)
        same = same_cell()
        for part, ref in ((wide[:S], wh_ref), (wide[S:], wl_ref)):
            tall = jnp.broadcast_to(part[:, None, :], (S, SUB, R)).reshape(R, R)
            ref[...] = jnp.where(same, tall, 0.0).astype(BF16)

    c = pl.program_id(0)
    levels = out_ref.shape[2]
    cut = 2 * PAIR // 2
    for k in range(levels):
        z = pl.program_id(1) * levels + k
        edge = 20 + 2 * c + jnp.where(z == NZ - 1, 1, 0)
        place = jnp.where(c == 2, 12 + z, jnp.where((z == 0) | (z == NZ - 1), edge, c * 6 + z - 1))
        columns = pl.ds(pl.multiple_of(place * PAIR, PAIR), PAIR)
        for low, up, depth in ((0, cut, cut), (cut, R, R)):
            wh, wl = wh_ref[low:up, :depth], wl_ref[low:up, :depth]
            h, l = h_ref[:depth, columns], l_ref[:depth, columns]
            part = (
                jnp.dot(wh, h, preferred_element_type=F32)
                + jnp.dot(wl, h, preferred_element_type=F32)
                + jnp.dot(wh * jnp.asarray(0.5, BF16), l, preferred_element_type=F32)
            )
            for half in range(2):
                tile = part[:, half * NX : (half + 1) * NX].reshape((up - low) // SUB, SUB, NX)
                out_ref[0, low // SUB : up // SUB, k, half * SUB : (half + 1) * SUB, :] = tile


def modes_and_factor(gram, high, low, count):
    levels = 2
    gram, high, low = in_vmem(gram, high, low)
    return pl.pallas_call(
        functools.partial(modes_kernel, count),
        name="modes",
        grid=(3, NZ // levels),
        out_shape=(
            jax.ShapeDtypeStruct((3, S, NZ, NY, NX), F32),
            jax.ShapeDtypeStruct((S, S), F32),
        ),
        in_specs=[vmem_spec()] * 3,
        out_specs=(
            pl.BlockSpec((1, S, levels, NY, NX), lambda c, z: (c, 0, z, 0, 0)),
            pl.BlockSpec((S, S), lambda c, z: (0, 0)),
        ),
        scratch_shapes=[pltpu.VMEM((R, R), BF16), pltpu.VMEM((R, R), BF16)],
        compiler_params=params(24),
    )(gram, high, low)


def ring(axis, shift):
    count = lax.axis_size(axis)
    return [(i, (i + shift) % count) for i in range(count)]


def total_over_devices(gram):
    gram = gram + lax.ppermute(gram, "span", ring("span", 1))
    gram = gram + lax.ppermute(gram, "vert", [(i, i ^ 1) for i in range(4)])
    gram = gram + lax.ppermute(gram, "vert", [(i, i ^ 3) for i in range(4)])
    for flip in (1, 3, 4, 12):
        gram = gram + lax.ppermute(gram, "stream", [(i, i ^ flip) for i in range(16)])
    return gram


def per_device(velocity):
    v = velocity.reshape(3, S, ROWS, NX)
    head, tail = vertical_faces(v)
    below = lax.ppermute(tail, "vert", ring("vert", 1))
    above = lax.ppermute(head, "vert", ring("vert", -1))
    block, xs, ys = side_faces(v)
    hy = lax.ppermute(ys, "span", ring("span", 1))
    left = lax.ppermute(xs, "stream", ring("stream", 1))
    right = lax.ppermute(xs, "stream", ring("stream", -1))
    high, low, part, acc = interior(block, hy, left, right)
    high, low, gram = boundary(block, part, below, above, acc, high, low)
    gram = total_over_devices(gram)
    devices = lax.axis_size("stream") * lax.axis_size("span") * lax.axis_size("vert")
    count = float(3 * NZ * NY * NX * devices)
    return modes_and_factor(gram, high, low, count)


def solution(mesh):
    spec = P(None, None, "vert", "span", "stream")
    return jax.shard_map(per_device, mesh=mesh, in_specs=(spec,), out_specs=(spec, P()), check_vma=False)
```

profile of v0, /device:TPU:0, one launch (start us, length us, event | category | flops | bytes accessed | tf_op | source)
XLA Modules:
  0.0 82.3 jit_solution(13446168835087568623)
XLA Ops:
  0.6 0.0 copy-start
  0.6 3.7 %copy-done = f32[3,48,8,16,128]{4,3,2,1,0:T(8,128)S(1)} copy-done((f32[3,48,8,16,128]{4,3,2,1,0:T(8,128)S(1)}, f32[3,48,8,16,128]{4,3,2,1,0:T(8,128)}, u32[]{:S(2)}) %copy-start) | copy-done | bytes 9437208
  4.3 0.0 copy-start.1
  4.3 0.3 vertical_faces.1
  4.6 1.6 %collective-permute-start.3 = (f32[2,48,16,128]{3,2,1,0:T(8,128)S(1)}, f32[2,48,16,128]{3,2,1,0:T(8,128)S(1)}, u32[]{:S(2)}, u32[]{:S(2)}) collective-permute-start(f32[2,48,16,128]{3,2,1,0:T(8,128)S(1)} %get-tuple-element.18), channel_id=1, source_target_pairs={{0,1},{1,2},{2,3},{3,0},{4,5},{5,6},{6,7},{7,4},{8,9},{9,10},{10,1... | collective-permute-start | bytes 2359304 | tf_op jit(solution)/shard_map/ppermute | solution.py:362
  6.2 1.7 %collective-permute-start.4 = (f32[2,48,16,128]{3,2,1,0:T(8,128)S(1)}, f32[2,48,16,128]{3,2,1,0:T(8,128)S(1)}, u32[]{:S(2)}, u32[]{:S(2)}) collective-permute-start(f32[2,48,16,128]{3,2,1,0:T(8,128)S(1)} %get-tuple-element.19), channel_id=1, source_target_pairs={{0,3},{1,0},{2,1},{3,2},{4,7},{5,4},{6,5},{7,6},{8,11},{9,8},{10,9... | collective-permute-start | bytes 2359304 | tf_op jit(solution)/shard_map/ppermute | solution.py:363
  7.9 0.1 copy-done.1
  8.0 3.6 %side_faces.1 = (f32[3,48,128,128]{3,2,1,0:T(8,128)S(1)}, f32[2,128,128]{2,1,0:T(8,128)S(1)}, f32[2,48,8,128]{3,2,1,0:T(8,128)S(1)}) custom-call(f32[3,48,128,128]{3,2,1,0:T(8,128)S(1)} %bitcast.2), custom_call_target="tpu_custom_call" | custom-call | tf_op jit(solution)/shard_map/side_faces/pallas_call | solution.py:96
  11.6 0.1 collective-permute-start
  11.7 6.6 %collective-permute-start.2 = (f32[2,128,128]{2,1,0:T(8,128)S(1)}, f32[2,128,128]{2,1,0:T(8,128)S(1)}, u32[]{:S(2)}, u32[]{:S(2)}) collective-permute-start(f32[2,128,128]{2,1,0:T(8,128)S(1)} %get-tuple-element.16), channel_id=1, source_target_pairs={{0,120},{8,0},{16,8},{24,16},{32,24},{40,32},{48,40},{56,48},{64,5... | collective-permute-start | bytes 393224 | tf_op jit(solution)/shard_map/ppermute | solution.py:367
  18.3 0.0 collective-permute-start.1
  18.4 3.4 %collective-permute-done.2.right_ref = f32[2,128,128]{2,1,0:T(8,128)S(1)} collective-permute-done((f32[2,128,128]{2,1,0:T(8,128)S(1)}, f32[2,128,128]{2,1,0:T(8,128)S(1)}, u32[]{:S(2)}, u32[]{:S(2)}) %collective-permute-start.2) | collective-permute-done | bytes 131104 | tf_op jit(solution)/shard_map/ppermute | solution.py:367
  21.7 5.5 %collective-permute-done.1.left_ref = f32[2,128,128]{2,1,0:T(8,128)S(1)} collective-permute-done((f32[2,128,128]{2,1,0:T(8,128)S(1)}, f32[2,128,128]{2,1,0:T(8,128)S(1)}, u32[]{:S(2)}, u32[]{:S(2)}) %collective-permute-start.1) | collective-permute-done | bytes 131104 | tf_op jit(solution)/shard_map/ppermute | solution.py:366
  27.2 0.0 collective-permute-done.hy_ref
  27.2 11.9 %interior.1 = (bf16[384,6144]{1,0:T(8,128)(2,1)S(1)}, bf16[384,6144]{1,0:T(8,128)(2,1)S(1)}, f32[2,2,48,16,128]{4,3,2,1,0:T(8,128)S(1)}, f32[384,384]{1,0:T(8,128)S(1)}) custom-call(f32[3,48,128,128]{3,2,1,0:T(8,128)S(1)} %get-tuple-element.14.v_ref, f32[2,48,8,128]{3,2,1,0:T(8,128)S(1)} %collective-permute-done.hy_ref, ...), custom_call_target="tpu_custom_call" | custom-call | flops 3019898880 | bytes 31457280 | tf_op jit(solution)/shard_map/interior/pallas_call | solution.py:202
  39.1 0.0 collective-permute-done.3.below_ref
  39.1 0.0 collective-permute-done.4.above_ref
  39.1 1.6 %boundary.1 = (bf16[384,6144]{1,0:T(8,128)(2,1)S(1)}, bf16[384,6144]{1,0:T(8,128)(2,1)S(1)}, f32[48,128]{1,0:T(8,128)S(1)}) custom-call(f32[3,48,128,128]{3,2,1,0:T(8,128)S(1)} %get-tuple-element.14.v_ref, f32[2,2,48,16,128]{4,3,2,1,0:T(8,128)S(1)} %get-tuple-element.17.part_ref, ...), custom_call_target="tpu_custom_call", output_to_operand_aliasing={{0}: (5, {}), {1}: (6, {})} | custom-call | tf_op jit(solution)/shard_map/boundary/pallas_call | solution.py:263
  40.7 0.0 collective-permute-start.5
  40.8 1.2 %collective-permute-done.5 = f32[48,128]{1,0:T(8,128)S(1)} collective-permute-done((f32[48,128]{1,0:T(8,128)S(1)}, f32[48,128]{1,0:T(8,128)S(1)}, u32[]{:S(2)}, u32[]{:S(2)}) %collective-permute-start.5) | collective-permute-done | bytes 24608 | tf_op jit(solution)/shard_map/ppermute | solution.py:351
  41.9 1.5 %collective-permute-start.6 = (f32[48,128]{1,0:T(8,128)S(1)}, f32[48,128]{1,0:T(8,128)S(1)}, u32[]{:S(2)}, u32[]{:S(2)}) collective-permute-start(f32[48,128]{1,0:T(8,128)S(1)} %add.21), channel_id=1, source_target_pairs={{0,1},{1,0},{2,3},{3,2},{4,5},{5,4},{6,7},{7,6},{8,9},{9,8},{10,11... | collective-permute-start | bytes 73736 | tf_op jit(solution)/shard_map/ppermute | solution.py:352
  43.4 2.3 %collective-permute-done.6 = f32[48,128]{1,0:T(8,128)S(1)} collective-permute-done((f32[48,128]{1,0:T(8,128)S(1)}, f32[48,128]{1,0:T(8,128)S(1)}, u32[]{:S(2)}, u32[]{:S(2)}) %collective-permute-start.6) | collective-permute-done | bytes 24608 | tf_op jit(solution)/shard_map/ppermute | solution.py:352
  45.8 2.8 %collective-permute-start.7 = (f32[48,128]{1,0:T(8,128)S(1)}, f32[48,128]{1,0:T(8,128)S(1)}, u32[]{:S(2)}, u32[]{:S(2)}) collective-permute-start(f32[48,128]{1,0:T(8,128)S(1)} %add.22), channel_id=1, source_target_pairs={{0,3},{1,2},{2,1},{3,0},{4,7},{5,6},{6,5},{7,4},{8,11},{9,10},{10,... | collective-permute-start | bytes 73736 | tf_op jit(solution)/shard_map/ppermute | solution.py:353
  48.5 2.3 %collective-permute-done.7 = f32[48,128]{1,0:T(8,128)S(1)} collective-permute-done((f32[48,128]{1,0:T(8,128)S(1)}, f32[48,128]{1,0:T(8,128)S(1)}, u32[]{:S(2)}, u32[]{:S(2)}) %collective-permute-start.7) | collective-permute-done | bytes 24608 | tf_op jit(solution)/shard_map/ppermute | solution.py:353
  50.8 0.0 collective-permute-start.8
  50.8 3.8 %collective-permute-done.8 = f32[48,128]{1,0:T(8,128)S(1)} collective-permute-done((f32[48,128]{1,0:T(8,128)S(1)}, f32[48,128]{1,0:T(8,128)S(1)}, u32[]{:S(2)}, u32[]{:S(2)}) %collective-permute-start.8) | collective-permute-done | bytes 24608 | tf_op jit(solution)/shard_map/ppermute | solution.py:355
  54.6 0.0 collective-permute-start.9
  54.7 5.0 %collective-permute-done.9 = f32[48,128]{1,0:T(8,128)S(1)} collective-permute-done((f32[48,128]{1,0:T(8,128)S(1)}, f32[48,128]{1,0:T(8,128)S(1)}, u32[]{:S(2)}, u32[]{:S(2)}) %collective-permute-start.9) | collective-permute-done | bytes 24608 | tf_op jit(solution)/shard_map/ppermute | solution.py:355
  59.7 0.0 collective-permute-start.10
  59.7 3.8 %collective-permute-done.10 = f32[48,128]{1,0:T(8,128)S(1)} collective-permute-done((f32[48,128]{1,0:T(8,128)S(1)}, f32[48,128]{1,0:T(8,128)S(1)}, u32[]{:S(2)}, u32[]{:S(2)}) %collective-permute-start.10) | collective-permute-done | bytes 24608 | tf_op jit(solution)/shard_map/ppermute | solution.py:355
  63.5 0.0 collective-permute-start.11
  63.5 5.0 %collective-permute-done.11 = f32[48,128]{1,0:T(8,128)S(1)} collective-permute-done((f32[48,128]{1,0:T(8,128)S(1)}, f32[48,128]{1,0:T(8,128)S(1)}, u32[]{:S(2)}, u32[]{:S(2)}) %collective-permute-start.11) | collective-permute-done | bytes 24608 | tf_op jit(solution)/shard_map/ppermute | solution.py:355
  68.6 13.8 %modes.1 = (f32[3,48,8,16,128]{4,3,2,1,0:T(8,128)}, f32[48,48]{1,0:T(8,128)}) custom-call(f32[48,128]{1,0:T(8,128)S(1)} %add.27.gram_ref, bf16[384,6144]{1,0:T(8,128)(2,1)S(1)} %get-tuple-element.24.h_ref, bf16[384,6144]{1,0:T(8,128)(2,1)S(1)} %get-tuple-element.25.l_ref), custom_call_target="tpu_custom_call" | custom-call | tf_op jit(solution)/shard_map/modes/pallas_call | solution.py:327
  (7 shorter events, 0.0 us)
Async XLA Ops:
  0.6 3.7 %copy-start = (f32[3,48,8,16,128]{4,3,2,1,0:T(8,128)S(1)}, f32[3,48,8,16,128]{4,3,2,1,0:T(8,128)}, u32[]{:S(2)}) copy-start(f32[3,48,8,16,128]{4,3,2,1,0:T(8,128)} %param.1) | copy-start | bytes 28311556
  4.3 3.7 %copy-start.1 = (f32[3,48,8,16,128]{4,3,2,1,0:T(8,128)S(1)}, f32[3,48,8,16,128]{4,3,2,1,0:T(8,128)}, u32[]{:S(2)}) copy-start(f32[3,48,8,16,128]{4,3,2,1,0:T(8,128)} %param.1) | copy-start | bytes 28311556
  4.6 34.5 %collective-permute-start.3 = (f32[2,48,16,128]{3,2,1,0:T(8,128)S(1)}, f32[2,48,16,128]{3,2,1,0:T(8,128)S(1)}, u32[]{:S(2)}, u32[]{:S(2)}) collective-permute-start(f32[2,48,16,128]{3,2,1,0:T(8,128)S(1)} %get-tuple-element.18), channel_id=1, source_target_pairs={{0,1},{1,2},{2,3},{3,0},{4,5},{5,6},{6,7},{7,4},{8,9},{9,10},{10,1... | collective-permute-start | bytes 2359304 | tf_op jit(solution)/shard_map/ppermute | solution.py:362
  6.2 32.9 %collective-permute-start.4 = (f32[2,48,16,128]{3,2,1,0:T(8,128)S(1)}, f32[2,48,16,128]{3,2,1,0:T(8,128)S(1)}, u32[]{:S(2)}, u32[]{:S(2)}) collective-permute-start(f32[2,48,16,128]{3,2,1,0:T(8,128)S(1)} %get-tuple-element.19), channel_id=1, source_target_pairs={{0,3},{1,0},{2,1},{3,2},{4,7},{5,4},{6,5},{7,6},{8,11},{9,8},{10,9... | collective-permute-start | bytes 2359304 | tf_op jit(solution)/shard_map/ppermute | solution.py:363
  11.6 15.6 %collective-permute-start = (f32[2,48,8,128]{3,2,1,0:T(8,128)S(1)}, f32[2,48,8,128]{3,2,1,0:T(8,128)S(1)}, u32[]{:S(2)}, u32[]{:S(2)}) collective-permute-start(f32[2,48,8,128]{3,2,1,0:T(8,128)S(1)} %get-tuple-element.15), channel_id=1, source_target_pairs={{0,4},{4,0},{1,5},{5,1},{2,6},{6,2},{3,7},{7,3},{8,12},{12,8},{9,1... | collective-permute-start | bytes 1179656 | tf_op jit(solution)/shard_map/ppermute | solution.py:365
  11.7 10.0 %collective-permute-start.2 = (f32[2,128,128]{2,1,0:T(8,128)S(1)}, f32[2,128,128]{2,1,0:T(8,128)S(1)}, u32[]{:S(2)}, u32[]{:S(2)}) collective-permute-start(f32[2,128,128]{2,1,0:T(8,128)S(1)} %get-tuple-element.16), channel_id=1, source_target_pairs={{0,120},{8,0},{16,8},{24,16},{32,24},{40,32},{48,40},{56,48},{64,5... | collective-permute-start | bytes 393224 | tf_op jit(solution)/shard_map/ppermute | solution.py:367
  18.3 8.9 %collective-permute-start.1 = (f32[2,128,128]{2,1,0:T(8,128)S(1)}, f32[2,128,128]{2,1,0:T(8,128)S(1)}, u32[]{:S(2)}, u32[]{:S(2)}) collective-permute-start(f32[2,128,128]{2,1,0:T(8,128)S(1)} %get-tuple-element.16), channel_id=1, source_target_pairs={{0,8},{8,16},{16,24},{24,32},{32,40},{40,48},{48,56},{56,64},{64,7... | collective-permute-start | bytes 393224 | tf_op jit(solution)/shard_map/ppermute | solution.py:366
  40.7 1.2 %collective-permute-start.5 = (f32[48,128]{1,0:T(8,128)S(1)}, f32[48,128]{1,0:T(8,128)S(1)}, u32[]{:S(2)}, u32[]{:S(2)}) collective-permute-start(f32[48,128]{1,0:T(8,128)S(1)} %get-tuple-element.23), channel_id=1, source_target_pairs={{0,4},{4,0},{1,5},{5,1},{2,6},{6,2},{3,7},{7,3},{8,12},{12,8},{9,1... | collective-permute-start | bytes 73736 | tf_op jit(solution)/shard_map/ppermute | solution.py:351
  41.9 3.8 %collective-permute-start.6 = (f32[48,128]{1,0:T(8,128)S(1)}, f32[48,128]{1,0:T(8,128)S(1)}, u32[]{:S(2)}, u32[]{:S(2)}) collective-permute-start(f32[48,128]{1,0:T(8,128)S(1)} %add.21), channel_id=1, source_target_pairs={{0,1},{1,0},{2,3},{3,2},{4,5},{5,4},{6,7},{7,6},{8,9},{9,8},{10,11... | collective-permute-start | bytes 73736 | tf_op jit(solution)/shard_map/ppermute | solution.py:352
  45.8 5.0 %collective-permute-start.7 = (f32[48,128]{1,0:T(8,128)S(1)}, f32[48,128]{1,0:T(8,128)S(1)}, u32[]{:S(2)}, u32[]{:S(2)}) collective-permute-start(f32[48,128]{1,0:T(8,128)S(1)} %add.22), channel_id=1, source_target_pairs={{0,3},{1,2},{2,1},{3,0},{4,7},{5,6},{6,5},{7,4},{8,11},{9,10},{10,... | collective-permute-start | bytes 73736 | tf_op jit(solution)/shard_map/ppermute | solution.py:353
  50.8 3.8 %collective-permute-start.8 = (f32[48,128]{1,0:T(8,128)S(1)}, f32[48,128]{1,0:T(8,128)S(1)}, u32[]{:S(2)}, u32[]{:S(2)}) collective-permute-start(f32[48,128]{1,0:T(8,128)S(1)} %add.23), channel_id=1, source_target_pairs={{0,8},{8,0},{16,24},{24,16},{32,40},{40,32},{48,56},{56,48},{64,72... | collective-permute-start | bytes 73736 | tf_op jit(solution)/shard_map/ppermute | solution.py:355
  54.6 5.0 %collective-permute-start.9 = (f32[48,128]{1,0:T(8,128)S(1)}, f32[48,128]{1,0:T(8,128)S(1)}, u32[]{:S(2)}, u32[]{:S(2)}) collective-permute-start(f32[48,128]{1,0:T(8,128)S(1)} %add.24), channel_id=1, source_target_pairs={{0,24},{8,16},{16,8},{24,0},{32,56},{40,48},{48,40},{56,32},{64,88... | collective-permute-start | bytes 73736 | tf_op jit(solution)/shard_map/ppermute | solution.py:355
  59.7 3.8 %collective-permute-start.10 = (f32[48,128]{1,0:T(8,128)S(1)}, f32[48,128]{1,0:T(8,128)S(1)}, u32[]{:S(2)}, u32[]{:S(2)}) collective-permute-start(f32[48,128]{1,0:T(8,128)S(1)} %add.25), channel_id=1, source_target_pairs={{0,32},{8,40},{16,48},{24,56},{32,0},{40,8},{48,16},{56,24},{64,96... | collective-permute-start | bytes 73736 | tf_op jit(solution)/shard_map/ppermute | solution.py:355
  63.5 5.0 %collective-permute-start.11 = (f32[48,128]{1,0:T(8,128)S(1)}, f32[48,128]{1,0:T(8,128)S(1)}, u32[]{:S(2)}, u32[]{:S(2)}) collective-permute-start(f32[48,128]{1,0:T(8,128)S(1)} %add.26), channel_id=1, source_target_pairs={{0,96},{8,104},{16,112},{24,120},{32,64},{40,72},{48,80},{56,88},{... | collective-permute-start | bytes 73736 | tf_op jit(solution)/shard_map/ppermute | solution.py:355
where the time goes:
time: 82.5 us; the launch traced here: 82.3 us
  waiting for transfers between devices  32.4 us (39%)
  Pallas kernels  31.1 us (38%)
  starting transfers between devices  14.3 us (17%)
  local copies, waits for them, and re-layouts  3.77 us (5%)
    ppermute x4, waiting for transfers between devices, total_over_devices(): lax.ppermute(gram, 'stream', [(i, i ^ flip) for i in range(16)])  17.7 us
    pallas_call x1, Pallas kernels, modes_and_factor(): pl.pallas_call(functools.partial(modes_kernel, count), name='modes', grid...  13.8 us
    pallas_call x1, Pallas kernels, interior(): pl.pallas_call(interior_kernel, name='interior', out_shape=(pltpu.VMEM((R...  11.9 us
    ppermute x1, starting transfers between devices, per_device(): right = lax.ppermute(xs, 'stream', ring('stream', -1))  6.64 us
    ppermute x1, waiting for transfers between devices, per_device(): left = lax.ppermute(xs, 'stream', ring('stream', 1))  5.52 us
    unnamed x4, local copies, waits for them, and re-layouts  3.77 us
    pallas_call x1, Pallas kernels, side_faces(): pl.pallas_call(side_faces_kernel, name='side_faces', out_shape=(pltpu.VME...  3.61 us
    ppermute x1, waiting for transfers between devices, per_device(): right = lax.ppermute(xs, 'stream', ring('stream', -1))  3.36 us
  transfers between devices with their start and end apart: 12, of which 9 were waited for; matrix products, arithmetic and copies ran while one was open for 0% of the time, Pallas kernels for 19%

commit v1 on v0

v1 whole, which is shorter than its diff:
```python
import functools

import jax
import jax.numpy as jnp
from jax import lax
from jax.experimental import pallas as pl
from jax.experimental.pallas import tpu as pltpu
from jax.sharding import PartitionSpec as P

F32, BF16 = jnp.float32, jnp.bfloat16
HIGH = lax.Precision.HIGHEST
S, NZ, NY, NX = 48, 8, 16, 128
ROWS = NZ * NY
SUB = 8
R = S * SUB
PAIR = 2 * NX
MIB = 1 << 20
NT = (((1,), (1,)), ((), ()))


def any_spec():
    return pl.BlockSpec(memory_space=pl.ANY)


def vmem_spec():
    return pl.BlockSpec(memory_space=pltpu.VMEM)


def params(limit):
    return pltpu.CompilerParams(vmem_limit_bytes=limit * MIB)


def in_vmem(*arrays):
    return [pltpu.with_memory_space_constraint(a, pltpu.VMEM) for a in arrays]


def in_hbm(array):
    return pltpu.with_memory_space_constraint(array, pltpu.HBM)


def vertical_faces_kernel(v_ref, head_ref, tail_ref, sems):
    low = pltpu.make_async_copy(v_ref.at[0:2, :, pl.ds(0, NY)], head_ref, sems.at[0])
    high = pltpu.make_async_copy(v_ref.at[0:2, :, pl.ds(ROWS - NY, NY)], tail_ref, sems.at[1])
    low.start()
    high.start()
    low.wait()
    high.wait()


def vertical_faces(v):
    face = pltpu.VMEM((2, S, NY, NX), F32)
    return pl.pallas_call(
        vertical_faces_kernel,
        name="vertical_faces",
        out_shape=(face, face),
        in_specs=[any_spec()],
        out_specs=(vmem_spec(), vmem_spec()),
        scratch_shapes=[pltpu.SemaphoreType.DMA((2,))],
        compiler_params=params(8),
    )(in_hbm(v))


def side_faces_kernel(block_ref, x_ref, y_ref):
    lane = lax.broadcasted_iota(jnp.int32, (NY, NX), 1) // 2
    for c in (1, 2):

        def pack(z, carry, c=c):
            rows = pl.ds(pl.multiple_of(z * NY, NY), NY)
            packed = jnp.zeros((NY, NX), F32)
            for s in range(S):
                turned = pltpu.roll(block_ref[c, s, rows, :], 2 * s + 1, axis=1)
                packed = jnp.where(lane == s, turned, packed)
            x_ref[c - 1, rows, :] = packed
            return carry

        lax.fori_loop(0, NZ, pack, 0)
    first = lax.axis_index("span") == 0
    for k, c in enumerate((0, 2)):
        for s in range(S):
            high = block_ref[c, s, pl.ds(NY - 1, NZ, stride=NY), :]
            low = block_ref[c, s, pl.ds(0, NZ, stride=NY), :]
            y_ref[k, s] = jnp.where(first, high, low)


def side_faces(block):
    return pl.pallas_call(
        side_faces_kernel,
        name="side_faces",
        out_shape=(
            pltpu.VMEM((2, ROWS, NX), F32),
            pltpu.VMEM((2, S, NZ, NX), F32),
        ),
        in_specs=[vmem_spec()],
        out_specs=(vmem_spec(), vmem_spec()),
        compiler_params=params(8),
    )(*in_vmem(block))


def split_store(first, second, pair, place, h_ref, l_ref):
    for half in range(2):
        rows = slice(half * SUB, (half + 1) * SUB)
        value = jnp.concatenate([first[rows], second[rows]], axis=0)
        high = value.astype(BF16)
        low = ((value - high.astype(F32)) * 2.0).astype(BF16)
        where = (place, pl.ds(pair * 2 * SUB, 2 * SUB), pl.ds(half * NX, NX))
        h_ref[where] = high
        l_ref[where] = low


def products(h_ref, l_ref, places):
    highs, lows = [h_ref[p] for p in places], [l_ref[p] for p in places]
    left, right = jnp.concatenate(highs + highs, axis=1), jnp.concatenate(highs + lows, axis=1)
    return lax.dot_general(left, right, NT, preferred_element_type=F32)


def level(z):
    return pl.ds(pl.multiple_of(z * NY, NY), NY)


def slope_z(v_ref, c, s, z):
    return v_ref[c, s, level(z + 1), :] - v_ref[c, s, level(z - 1), :]


def slope_y(v_ref, hy_ref, c, s, z):
    row = lax.broadcasted_iota(jnp.int32, (NY, NX), 0)
    first = lax.axis_index("span") == 0
    cells = v_ref[c, s, level(z), :]
    face = hy_ref[c // 2, s, pl.ds(z, 1), :]
    up = jnp.where(row == NY - 1, jnp.where(first, face, 0.0), pltpu.roll(cells, NY - 1, axis=0))
    down = jnp.where(row == 0, jnp.where(first, 0.0, face), pltpu.roll(cells, 1, axis=0))
    return up - down


def slope_x(v_ref, edge_ref, c, s, z):
    lane = lax.broadcasted_iota(jnp.int32, (NY, NX), 1)
    cells = v_ref[c, s, level(z), :]
    edge = edge_ref[c - 1, level(z), :]
    if s:
        edge = pltpu.roll(edge, NX - 2 * s, axis=1)
    up = jnp.where(lane == NX - 1, edge, pltpu.roll(cells, NX - 1, axis=1))
    down = jnp.where(lane == 0, edge, pltpu.roll(cells, 1, axis=1))
    return up - down


def send_out(places, scratch, refs, sems):
    for i, (a, b) in enumerate(zip(scratch, refs)):
        for p in places:
            pltpu.make_async_copy(a.at[p], b.at[p], sems.at[i]).start()


def wait_out(scratch, refs, sems):
    for i, (a, b) in enumerate(zip(scratch, refs)):
        pltpu.make_async_copy(a, b, sems.at[i]).wait()


def first_kernel(v_ref, hy_ref, h_out, l_out, part_ref, acc_ref, h_ref, l_ref, sems):
    def vorticity(z):
        for s in range(0, S, 2):
            pair = (0.5 * (slope_y(v_ref, hy_ref, 2, t, z) - slope_z(v_ref, 1, t, z)) for t in (s, s + 1))
            split_store(*pair, s // 2, z - 1, h_ref, l_ref)
        send_out([z - 1], (h_ref, l_ref), (h_out, l_out), sems)

    def step(z, carry):
        acc_ref[...] += products(h_ref, l_ref, [z - 2])
        vorticity(z)
        return carry

    acc_ref[...] = jnp.zeros_like(acc_ref)
    vorticity(1)
    lax.fori_loop(2, NZ - 1, step, 0)
    acc_ref[...] += products(h_ref, l_ref, [NZ - 3])

    def outer(k, carry):
        for s in range(S):
            part_ref[k, s] = slope_y(v_ref, hy_ref, 2, s, k * (NZ - 1))
        return carry

    lax.fori_loop(0, 2, outer, 0)
    wait_out((h_ref, l_ref), (h_out, l_out), sems)


def first_component(block, hy):
    half = pltpu.HBM((6, R, PAIR), BF16)
    return pl.pallas_call(
        first_kernel,
        name="first_component",
        out_shape=(half, half, pltpu.VMEM((2, S, NY, NX), F32), pltpu.VMEM((R, R), F32)),
        in_specs=[vmem_spec()] * 2,
        out_specs=(any_spec(), any_spec(), vmem_spec(), vmem_spec()),
        scratch_shapes=[pltpu.VMEM((6, R, PAIR), BF16)] * 2 + [pltpu.SemaphoreType.DMA((2,))],
        compiler_params=params(8),
        cost_estimate=pl.CostEstimate(flops=4 * R * R * 6 * PAIR, bytes_accessed=6 * MIB, transcendentals=0),
    )(*in_vmem(block, hy))


def rest_kernel(v_ref, hy_ref, left_ref, right_ref, old_ref, h_out, l_out, part_ref, acc_ref, edge_ref, h_ref, l_ref, sems):
    lane = lax.broadcasted_iota(jnp.int32, (NY, NX), 1)
    stream = lax.axis_index("stream")
    for c in range(2):
        for z in range(NZ):
            rows = pl.ds(z * NY, NY)
            before = jnp.where(stream > 0, left_ref[c, rows, :], 0.0)
            behind = jnp.where(stream < lax.axis_size("stream") - 1, right_ref[c, rows, :], 0.0)
            edge_ref[c, rows, :] = jnp.where(lane % 2 == 0, before, pltpu.roll(behind, NX - 2, axis=1))

    def second(z):
        for s in range(0, S, 2):
            pair = (0.5 * (slope_z(v_ref, 0, t, z) - slope_x(v_ref, edge_ref, 2, t, z)) for t in (s, s + 1))
            split_store(*pair, s // 2, z - 1, h_ref, l_ref)
        send_out([z - 1], (h_ref, l_ref), (h_out, l_out), sems)

    def third(z):
        for s in range(0, S, 2):
            pair = (
                0.5 * (slope_x(v_ref, edge_ref, 1, t, z) - slope_y(v_ref, hy_ref, 0, t, z)) for t in (s, s + 1)
            )
            split_store(*pair, s // 2, z + 6, h_ref, l_ref)
        send_out([z + 6], (h_ref, l_ref), (h_out, l_out), sems)

    def step(z, carry):
        acc_ref[...] += products(h_ref, l_ref, [z - 2, z + 5])
        second(z)
        third(z)
        return carry

    third(0)
    acc_ref[...] = old_ref[...] + products(h_ref, l_ref, [6])
    second(1)
    third(1)
    lax.fori_loop(2, NZ - 1, step, 0)
    acc_ref[...] += products(h_ref, l_ref, [NZ - 3, NZ + 4])
    third(NZ - 1)
    acc_ref[...] += products(h_ref, l_ref, [NZ + 5])

    def outer(k, carry):
        for s in range(S):
            part_ref[k, s] = slope_x(v_ref, edge_ref, 2, s, k * (NZ - 1))
        return carry

    lax.fori_loop(0, 2, outer, 0)
    wait_out((h_ref, l_ref), (h_out, l_out), sems)


def other_components(block, hy, left, right, acc):
    half = pltpu.HBM((14, R, PAIR), BF16)
    return pl.pallas_call(
        rest_kernel,
        name="other_components",
        out_shape=(half, half, pltpu.VMEM((2, S, NY, NX), F32), pltpu.VMEM((R, R), F32)),
        in_specs=[vmem_spec()] * 5,
        out_specs=(any_spec(), any_spec(), vmem_spec(), vmem_spec()),
        scratch_shapes=[pltpu.VMEM((2, ROWS, NX), F32)]
        + [pltpu.VMEM((14, R, PAIR), BF16)] * 2
        + [pltpu.SemaphoreType.DMA((2,))],
        compiler_params=params(12),
        cost_estimate=pl.CostEstimate(flops=4 * R * R * 14 * PAIR, bytes_accessed=12 * MIB, transcendentals=0),
    )(*in_vmem(block, hy, left, right, acc))


def lane_fold():
    shape = (R, NX)
    same = lax.broadcasted_iota(jnp.int32, shape, 0) // SUB == lax.broadcasted_iota(jnp.int32, shape, 1)
    return jnp.where(same, 1.0, 0.0)


def same_cell():
    return lax.broadcasted_iota(jnp.int32, (R, R), 0) % SUB == lax.broadcasted_iota(jnp.int32, (R, R), 1) % SUB


def boundary_kernel(
    v_ref, wy_ref, wx_ref, below_ref, above_ref, acc_ref, h_ref, l_ref, mine_ref, other_ref
):
    vert = lax.axis_index("vert")
    has_below, has_above = vert > 0, vert < lax.axis_size("vert") - 1

    def dz(c, s, k):
        if k:
            return jnp.where(has_above, above_ref[c, s], 0.0) - v_ref[c, s, pl.ds((NZ - 2) * NY, NY), :]
        return v_ref[c, s, pl.ds(NY, NY), :] - jnp.where(has_below, below_ref[c, s], 0.0)

    for k in range(2):
        for s in range(0, S, 2):
            split_store(
                *(0.5 * (wy_ref[k, t] - dz(1, t, k)) for t in (s, s + 1)),
                s // 2, k, h_ref, l_ref,
            )
            split_store(
                *(0.5 * (dz(0, t, k) - wx_ref[k, t]) for t in (s, s + 1)),
                s // 2, 2 + k, h_ref, l_ref,
            )
    total = acc_ref[...] + products(h_ref, l_ref, range(4))
    total = jnp.where(same_cell(), total, 0.0).reshape(S, SUB, R).sum(1)
    total = lax.dot_general(
        total, lane_fold(), (((1,), (0,)), ((), ())), precision=HIGH, preferred_element_type=F32
    )
    square = jnp.concatenate([total, jnp.zeros((NX - S, NX), F32)], axis=0)
    total = 0.5 * (total + square.T[:S])
    lane = lax.broadcasted_iota(jnp.int32, (SUB, NX), 1)
    groups = [total[g * SUB : (g + 1) * SUB] for g in range(S // SUB)]
    bottom = jnp.where(lane < 48, groups[4], pltpu.roll(groups[5], 48, axis=1))
    top = jnp.where(lane < 64, pltpu.roll(groups[2], 32, axis=1), pltpu.roll(groups[3], 64, axis=1))
    top = jnp.where(lane < 16, groups[0], jnp.where(lane < 32, pltpu.roll(groups[1], 16, axis=1), top))
    first = lax.axis_index("span") == 0
    mine_ref[...] = jnp.where(first, top, bottom)
    other_ref[...] = jnp.where(first, bottom, top)


def boundary(block, wy, wx, below, above, acc):
    half = pltpu.VMEM((4, R, PAIR), BF16)
    sums = pltpu.VMEM((SUB, NX), F32)
    return pl.pallas_call(
        boundary_kernel,
        name="boundary",
        out_shape=(half, half, sums, sums),
        in_specs=[vmem_spec()] * 6,
        out_specs=(vmem_spec(),) * 4,
        compiler_params=params(8),
    )(*in_vmem(block, wy, wx, below, above, acc))


def eliminate(work):
    row = lax.broadcasted_iota(jnp.int32, (SUB, NX), 0)

    def spread(part):
        return jnp.broadcast_to(part, (SUB, NX))

    width = SUB
    for start in range(0, S, width):
        home, base = start // SUB, start % SUB
        live = range(home, S // SUB)
        pivots = [spread(work[home][base + j : base + j + 1, :]) for j in range(width)]
        cols = [{g: spread(work[g][:, start + j : start + j + 1]) for g in live} for j in range(width)]
        heads = [[spread(cols[j][home][base + i : base + i + 1, :]) for j in range(width)] for i in range(width)]
        for i in range(width):
            scale = 1.0 / heads[i][i]
            for j in range(i + 1, width):
                ratio = heads[i][j] * scale
                pivots[j] = pivots[j] - ratio * pivots[i]
                for g in live:
                    cols[j][g] = cols[j][g] - ratio * cols[i][g]
                for k in range(j, width):
                    heads[j][k] = heads[j][k] - ratio * heads[i][k]
            for g in live:
                factor = cols[i][g] * scale
                if g == home:
                    factor = jnp.where(row > base + i, factor, 0.0)
                work[g] = work[g] - factor * pivots[i]
    return work


def modes_kernel(count, mine_ref, other_ref, edge_h_ref, edge_l_ref, *refs):
    parts, (out_ref, factor_ref, h_ref, l_ref, wide_ref, corner_ref, buffer, sems, in_sems) = refs[:4], refs[4:]
    loads, start = [], 0
    for k in range(2):
        width = parts[2 * k].shape[0]
        loads.append(
            [
                pltpu.make_async_copy(parts[2 * k + j], ref.at[pl.ds(start, width)], in_sems.at[2 * k + j])
                for j, ref in enumerate((h_ref, l_ref))
            ]
        )
        for load in loads[-1]:
            load.start()
        start += width
    cut = 2 * NX

    @pl.when(lax.axis_index("stream") >= 0)
    def _():
        first = lax.axis_index("span") == 0
        top = jnp.where(first, mine_ref[...], other_ref[...])
        bottom = jnp.where(first, other_ref[...], mine_ref[...])
        groups = [top, pltpu.roll(top, NX - 16, axis=1), pltpu.roll(top, NX - 32, axis=1)]
        groups += [pltpu.roll(top, NX - 64, axis=1), bottom, pltpu.roll(bottom, NX - 48, axis=1)]
        shape = (S, NX)
        row = lax.broadcasted_iota(jnp.int32, shape, 0)
        lane = lax.broadcasted_iota(jnp.int32, shape, 1)
        raw = jnp.concatenate(groups, axis=0) / count
        below = jnp.where(lane < row, raw, 0.0)
        square = jnp.concatenate([below, jnp.zeros((NX - S, NX), F32)], axis=0)
        work = jnp.where(lane <= row, raw, 0.0) + square.T[:S] + jnp.where(lane == row + NX // 2, 1.0, 0.0)
        work = jnp.concatenate(eliminate([work[g * SUB : (g + 1) * SUB] for g in range(S // SUB)]), axis=0)
        diagonal = jnp.sum(jnp.where(lane == row, work, 0.0), axis=1, keepdims=True)
        work = work * lax.rsqrt(diagonal)
        factor_ref[...] = jnp.where(lane >= row, work, 0.0)[:, :S]
        inverse = jnp.where(lane <= row, pltpu.roll(work, NX // 2, axis=1), 0.0)
        high = inverse.astype(BF16).astype(F32)
        both = jnp.concatenate([high, inverse - high], axis=0).astype(BF16)
        wide = lax.dot_general(both, lane_fold().astype(BF16), NT, preferred_element_type=F32)
        same = same_cell()
        tall_high, tall_low = (
            jnp.where(same, jnp.broadcast_to(part[:, None, :], (S, SUB, R)).reshape(R, R), 0.0)
            for part in (wide[:S], wide[S:])
        )
        half = 0.5 * tall_high
        wide_ref[...] = jnp.concatenate([m[:, :cut] for m in (tall_high, tall_low, half)], axis=1).astype(BF16)
        corner = jnp.concatenate(
            [
                jnp.concatenate([tall_high[cut:, cut:], half[cut:, cut:]], axis=1),
                jnp.concatenate([tall_low[cut:, cut:], jnp.zeros((R - cut, R - cut), F32)], axis=1),
            ],
            axis=0,
        )
        corner_ref[...] = corner.astype(BF16)

    slots = buffer.shape[0]

    group = 4

    def copy_out(place):
        q = place - group
        c = jnp.where(q < 0, place // 2, jnp.where(q < 6, 0, jnp.where(q < 12, 1, 2)))
        z = jnp.where(q < 0, place % 2 * (NZ - 1), jnp.where(q < 12, q % 6 + 1, q - 12))
        slot = place % slots
        return pltpu.make_async_copy(buffer.at[slot], out_ref.at[c, :, z], sems.at[slot])

    def apply(step, carry, source=None):
        first = step * group
        if source is None:
            source = (h_ref, l_ref)
            start = first - group

            @pl.when(step >= slots // group)
            def _():
                for k in range(group):
                    copy_out(first + k - slots).wait()
        else:
            start = 0

        for k in range(group):
            h, l = (ref[start + k] for ref in source)
            part = jnp.dot(
                wide_ref[...], jnp.concatenate([h[:cut], h[:cut], l[:cut]], axis=0), preferred_element_type=F32
            )
            last = jnp.dot(
                corner_ref[...], jnp.concatenate([h[cut:], l[cut:]], axis=0), preferred_element_type=F32
            )
            last = part[cut:] + last[: R - cut] + last[R - cut :]
            for value, low in ((part[:cut], 0), (last, cut // SUB)):
                rows = value.shape[0] // SUB
                for half in range(2):
                    tile = value[:, half * NX : (half + 1) * NX].reshape(rows, SUB, NX)
                    buffer[(first + k) % slots, low : low + rows, half * SUB : (half + 1) * SUB, :] = tile
        for k in range(group):
            copy_out(first + k).start()
        return carry

    lax.fori_loop(0, 1, lambda step, carry: apply(0, carry, (edge_h_ref, edge_l_ref)), 0)
    for pair, low, high in zip(loads, (1, 2), (2, 6)):
        for load in pair:
            load.wait()
        lax.fori_loop(low, high, apply, 0)
    for place in range(24 - slots, 24):
        copy_out(place).wait()


def modes_and_factor(mine, other, edge_halves, halves, count):
    return pl.pallas_call(
        functools.partial(modes_kernel, count),
        name="modes",
        out_shape=(
            pltpu.HBM((3, S, NZ, NY, NX), F32),
            jax.ShapeDtypeStruct((S, S), F32),
        ),
        in_specs=[vmem_spec()] * 4 + [any_spec()] * 4,
        out_specs=(any_spec(), vmem_spec()),
        scratch_shapes=[pltpu.VMEM((20, R, PAIR), BF16)] * 2
        + [pltpu.VMEM((R, 6 * NX), BF16), pltpu.VMEM((2 * NX, 2 * NX), BF16)]
        + [pltpu.VMEM((12, S, NY, NX), F32), pltpu.SemaphoreType.DMA((12,)), pltpu.SemaphoreType.DMA((4,))],
        compiler_params=params(24),
    )(*in_vmem(mine, other, *edge_halves), *(in_hbm(h) for h in halves))


def ring(axis, shift):
    count = lax.axis_size(axis)
    return [(i, (i + shift) % count) for i in range(count)]


def total_over_devices(mine, other):
    swap = ring("span", 1)
    mine = mine + lax.ppermute(other, "span", swap)
    axes = ("stream", "vert")
    peers = lax.axis_size(axes)
    mine = lax.all_to_all(jnp.broadcast_to(mine, (peers,) + mine.shape), axes, 0, 0).sum(0)
    return mine, lax.ppermute(mine, "span", swap)


def per_device(velocity):
    v = velocity.reshape(3, S, ROWS, NX)
    head, tail = vertical_faces(v)
    below = lax.ppermute(tail, "vert", ring("vert", 1))
    above = lax.ppermute(head, "vert", ring("vert", -1))
    xs, ys = side_faces(v)
    hy = lax.ppermute(ys, "span", ring("span", 1))
    left = lax.ppermute(xs, "stream", ring("stream", 1))
    right = lax.ppermute(xs, "stream", ring("stream", -1))
    *head_halves, wy, acc = first_component(v, hy)
    *rest_halves, wx, acc = other_components(v, hy, left, right, acc)
    *edge_halves, mine, other = boundary(v, wy, wx, below, above, acc)
    mine, other = total_over_devices(mine, other)
    devices = lax.axis_size("stream") * lax.axis_size("span") * lax.axis_size("vert")
    count = float(3 * NZ * NY * NX * devices)
    return modes_and_factor(mine, other, edge_halves, head_halves + rest_halves, count)


def solution(mesh):
    spec = P(None, None, "vert", "span", "stream")
    return jax.shard_map(per_device, mesh=mesh, in_specs=(spec,), out_specs=(spec, P()), check_vma=False)
```

time: 82.5 us -> 60.9 us (0.74)
  the two profiles are of different devices: /device:TPU:0 before, /device:TPU:1 now
where the time goes in v1:
time: 60.9 us; the launch traced here: 60.7 us
  Pallas kernels  26 us (43%)
  blocking collectives  14.1 us (23%)
  starting transfers between devices  13.9 us (23%)
  waiting for transfers between devices  5.84 us (10%)
  between operations  0.7 us (1%)
    all_to_all x1, blocking collectives, total_over_devices(): lax.all_to_all(jnp.broadcast_to(mine, (peers,) + mine.shape), axes, 0, 0)  14.1 us
    pallas_call x1, Pallas kernels, modes_and_factor(): pl.pallas_call(functools.partial(modes_kernel, count), name='modes', out_...  9.61 us
    pallas_call x1, Pallas kernels, other_components(): pl.pallas_call(rest_kernel, name='other_components', out_shape=(half, hal...  6.36 us
    ppermute x1, starting transfers between devices, per_device(): right = lax.ppermute(xs, 'stream', ring('stream', -1))  6.31 us
    ppermute x1, waiting for transfers between devices, per_device(): left = lax.ppermute(xs, 'stream', ring('stream', 1))  4.18 us
    pallas_call x1, Pallas kernels, first_component(): pl.pallas_call(first_kernel, name='first_component', out_shape=(half, hal...  3.85 us
    pallas_call x1, Pallas kernels, side_faces(): pl.pallas_call(side_faces_kernel, name='side_faces', out_shape=(pltpu.VME...  2.93 us
    ppermute x1, starting transfers between devices, per_device(): below = lax.ppermute(tail, 'vert', ring('vert', 1))  2.11 us
  transfers between devices with their start and end apart: 7, of which 3 were waited for; matrix products, arithmetic and copies ran while one was open for 0% of the time, Pallas kernels for 22%

profile of v1, /device:TPU:1, one launch (start us, length us, event | category | flops | bytes accessed | tf_op | source)
XLA Modules:
  0.0 60.7 jit_solution(3053393779089393575)
XLA Ops:
  0.6 0.0 copy-start
  0.6 1.5 %vertical_faces.1 = (f32[2,48,16,128]{3,2,1,0:T(8,128)S(1)}, f32[2,48,16,128]{3,2,1,0:T(8,128)S(1)}) custom-call(f32[3,48,128,128]{3,2,1,0:T(8,128)} %bitcast.1), custom_call_target="tpu_custom_call" | custom-call | tf_op jit(solution)/shard_map/vertical_faces/pallas_call | solution.py:52
  2.2 2.1 %collective-permute-start.3 = (f32[2,48,16,128]{3,2,1,0:T(8,128)S(1)}, f32[2,48,16,128]{3,2,1,0:T(8,128)S(1)}, u32[]{:S(2)}, u32[]{:S(2)}) collective-permute-start(f32[2,48,16,128]{3,2,1,0:T(8,128)S(1)} %get-tuple-element.23), channel_id=1, source_target_pairs={{0,1},{1,2},{2,3},{3,0},{4,5},{5,6},{6,7},{7,4},{8,9},{9,10},{10,1... | collective-permute-start | bytes 2359304 | tf_op jit(solution)/shard_map/ppermute | solution.py:490
  4.3 1.3 %collective-permute-start.4 = (f32[2,48,16,128]{3,2,1,0:T(8,128)S(1)}, f32[2,48,16,128]{3,2,1,0:T(8,128)S(1)}, u32[]{:S(2)}, u32[]{:S(2)}) collective-permute-start(f32[2,48,16,128]{3,2,1,0:T(8,128)S(1)} %get-tuple-element.24), channel_id=1, source_target_pairs={{0,3},{1,0},{2,1},{3,2},{4,7},{5,4},{6,5},{7,6},{8,11},{9,8},{10,9... | collective-permute-start | bytes 2359304 | tf_op jit(solution)/shard_map/ppermute | solution.py:491
  5.7 0.0 copy-done
  5.7 2.9 %side_faces.1 = (f32[2,128,128]{2,1,0:T(8,128)S(1)}, f32[2,48,8,128]{3,2,1,0:T(8,128)S(1)}) custom-call(f32[3,48,128,128]{3,2,1,0:T(8,128)S(1)} %bitcast.2), custom_call_target="tpu_custom_call" | custom-call | tf_op jit(solution)/shard_map/side_faces/pallas_call | solution.py:86
  8.6 1.3 %collective-permute-start = (f32[2,48,8,128]{3,2,1,0:T(8,128)S(1)}, f32[2,48,8,128]{3,2,1,0:T(8,128)S(1)}, u32[]{:S(2)}, u32[]{:S(2)}) collective-permute-start(f32[2,48,8,128]{3,2,1,0:T(8,128)S(1)} %get-tuple-element.18), channel_id=1, source_target_pairs={{0,4},{4,0},{1,5},{5,1},{2,6},{6,2},{3,7},{7,3},{8,12},{12,8},{9,1... | collective-permute-start | bytes 1179656 | tf_op jit(solution)/shard_map/ppermute | solution.py:493
  9.9 6.3 %collective-permute-start.2 = (f32[2,128,128]{2,1,0:T(8,128)S(1)}, f32[2,128,128]{2,1,0:T(8,128)S(1)}, u32[]{:S(2)}, u32[]{:S(2)}) collective-permute-start(f32[2,128,128]{2,1,0:T(8,128)S(1)} %get-tuple-element.20), channel_id=1, source_target_pairs={{0,120},{8,0},{16,8},{24,16},{32,24},{40,32},{48,40},{56,48},{64,5... | collective-permute-start | bytes 393224 | tf_op jit(solution)/shard_map/ppermute | solution.py:495
  16.2 0.0 collective-permute-start.1
  16.3 0.0 collective-permute-done.hy_ref
  16.3 3.8 %first_component.1 = (bf16[6,384,256]{2,1,0:T(8,128)(2,1)}, bf16[6,384,256]{2,1,0:T(8,128)(2,1)}, f32[2,48,16,128]{3,2,1,0:T(8,128)S(1)}, f32[384,384]{1,0:T(8,128)S(1)}) custom-call(f32[3,48,128,128]{3,2,1,0:T(8,128)S(1)} %bitcast.3, f32[2,48,8,128]{3,2,1,0:T(8,128)S(1)} %collective-permute-done.hy_ref), custom_call_target="tpu_custom_call" | custom-call | flops 905969664 | bytes 6291456 | tf_op jit(solution)/shard_map/first_component/pallas_call | solution.py:184
  20.1 0.0 collective-permute-done.2.right_ref
  20.1 4.2 %collective-permute-done.1.left_ref = f32[2,128,128]{2,1,0:T(8,128)S(1)} collective-permute-done((f32[2,128,128]{2,1,0:T(8,128)S(1)}, f32[2,128,128]{2,1,0:T(8,128)S(1)}, u32[]{:S(2)}, u32[]{:S(2)}) %collective-permute-start.1) | collective-permute-done | bytes 131104 | tf_op jit(solution)/shard_map/ppermute | solution.py:494
  24.3 6.4 %other_components.1 = (bf16[14,384,256]{2,1,0:T(8,128)(2,1)}, bf16[14,384,256]{2,1,0:T(8,128)(2,1)}, f32[2,48,16,128]{3,2,1,0:T(8,128)S(1)}, f32[384,384]{1,0:T(8,128)S(1)}) custom-call(f32[3,48,128,128]{3,2,1,0:T(8,128)S(1)} %bitcast.4, f32[2,48,8,128]{3,2,1,0:T(8,128)S(1)} %collective-permute-done.hy_ref, ...), custom_call_target="tpu_custom_call" | custom-call | flops 2113929216 | bytes 12582912 | tf_op jit(solution)/shard_map/other_components/pallas_call | solution.py:246
  30.7 0.0 collective-permute-done.3.below_ref
  30.7 0.0 collective-permute-done.4.above_ref
  30.7 1.7 %boundary.1 = (bf16[4,384,256]{2,1,0:T(8,128)(2,1)S(1)}, bf16[4,384,256]{2,1,0:T(8,128)(2,1)S(1)}, f32[8,128]{1,0:T(8,128)S(1)}, f32[8,128]{1,0:T(8,128)S(1)}) custom-call(f32[3,48,128,128]{3,2,1,0:T(8,128)S(1)} %bitcast.5, f32[2,48,16,128]{3,2,1,0:T(8,128)S(1)} %get-tuple-element.19.wy_ref, f32[2,48,16,128]{3,2,1,0:T(8,128)S(1)} %get-tuple-element.22.wx_ref, ...), custom_call_target="tpu_custom_call" | custom-call | tf_op jit(solution)/shard_map/boundary/pallas_call | solution.py:311
  32.4 1.2 %collective-permute-start.5 = (f32[8,128]{1,0:T(8,128)S(1)}, f32[8,128]{1,0:T(8,128)S(1)}, u32[]{:S(2)}, u32[]{:S(2)}) collective-permute-start(f32[8,128]{1,0:T(8,128)S(1)} %get-tuple-element.27), channel_id=1, source_target_pairs={{0,4},{4,0},{1,5},{5,1},{2,6},{6,2},{3,7},{7,3},{8,12},{12,8},{9,1... | collective-permute-start | bytes 12296 | tf_op jit(solution)/shard_map/ppermute | solution.py:480
  33.6 0.8 %collective-permute-done.5 = f32[8,128]{1,0:T(8,128)S(1)} collective-permute-done((f32[8,128]{1,0:T(8,128)S(1)}, f32[8,128]{1,0:T(8,128)S(1)}, u32[]{:S(2)}, u32[]{:S(2)}) %collective-permute-start.5) | collective-permute-done | bytes 4128 | tf_op jit(solution)/shard_map/ppermute | solution.py:480
  34.5 14.1 %all_to_all.5 = f32[64,8,128]{2,1,0:T(8,128)S(1)} all-to-all(f32[64,8,128]{2,1,0:T(8,128)S(1)} %broadcast_in_dim.3), channel_id=1, replica_groups=mesh['stream'=16,'span'=2,'vert'=4] {'stream','vert'}, dimensions={0} | all-to-all | bytes 524288 | tf_op jit(solution)/shard_map/all_to_all | solution.py:483
  48.6 0.1 reduce_sum.9.mine_ref
  48.7 1.6 %collective-permute-start.6 = (f32[8,128]{1,0:T(8,128)S(1)}, f32[8,128]{1,0:T(8,128)S(1)}, u32[]{:S(2)}, u32[]{:S(2)}) collective-permute-start(f32[8,128]{1,0:T(8,128)S(1)} %reduce_sum.9.mine_ref), channel_id=1, source_target_pairs={{0,4},{4,0},{1,5},{5,1},{2,6},{6,2},{3,7},{7,3},{8,12},{12,8},{9,1... | collective-permute-start | bytes 12296 | tf_op jit(solution)/shard_map/ppermute | solution.py:484
  50.3 0.8 %collective-permute-done.6.other_ref = f32[8,128]{1,0:T(8,128)S(1)} collective-permute-done((f32[8,128]{1,0:T(8,128)S(1)}, f32[8,128]{1,0:T(8,128)S(1)}, u32[]{:S(2)}, u32[]{:S(2)}) %collective-permute-start.6) | collective-permute-done | bytes 4128 | tf_op jit(solution)/shard_map/ppermute | solution.py:484
  51.1 9.6 %modes.1 = (f32[3,48,8,16,128]{4,3,2,1,0:T(8,128)}, f32[48,48]{1,0:T(8,128)}) custom-call(f32[8,128]{1,0:T(8,128)S(1)} %reduce_sum.9.mine_ref, f32[8,128]{1,0:T(8,128)S(1)} %collective-permute-done.6.other_ref, bf16[4,384,256]{2,1,0:T(8,128)(2,1)S(1)} %get-tuple-element.28.edge_h_ref, bf16[4,384,256]{2,1,0:T(8,128)(2,1)S(1)} %get-tuple-element.29.edge_l_ref, ...), custom_call_target="tpu_custom_call" | custom-call | tf_op jit(solution)/shard_map/modes/pallas_call | solution.py:457
  (2 shorter events, 0.0 us)
Async XLA Ops:
  0.6 5.0 %copy-start = (f32[3,48,8,16,128]{4,3,2,1,0:T(8,128)S(1)}, f32[3,48,8,16,128]{4,3,2,1,0:T(8,128)}, u32[]{:S(2)}) copy-start(f32[3,48,8,16,128]{4,3,2,1,0:T(8,128)} %param.1) | copy-start | bytes 28311556
  2.2 28.5 %collective-permute-start.3 = (f32[2,48,16,128]{3,2,1,0:T(8,128)S(1)}, f32[2,48,16,128]{3,2,1,0:T(8,128)S(1)}, u32[]{:S(2)}, u32[]{:S(2)}) collective-permute-start(f32[2,48,16,128]{3,2,1,0:T(8,128)S(1)} %get-tuple-element.23), channel_id=1, source_target_pairs={{0,1},{1,2},{2,3},{3,0},{4,5},{5,6},{6,7},{7,4},{8,9},{9,10},{10,1... | collective-permute-start | bytes 2359304 | tf_op jit(solution)/shard_map/ppermute | solution.py:490
  4.3 26.4 %collective-permute-start.4 = (f32[2,48,16,128]{3,2,1,0:T(8,128)S(1)}, f32[2,48,16,128]{3,2,1,0:T(8,128)S(1)}, u32[]{:S(2)}, u32[]{:S(2)}) collective-permute-start(f32[2,48,16,128]{3,2,1,0:T(8,128)S(1)} %get-tuple-element.24), channel_id=1, source_target_pairs={{0,3},{1,0},{2,1},{3,2},{4,7},{5,4},{6,5},{7,6},{8,11},{9,8},{10,9... | collective-permute-start | bytes 2359304 | tf_op jit(solution)/shard_map/ppermute | solution.py:491
  8.6 7.7 %collective-permute-start = (f32[2,48,8,128]{3,2,1,0:T(8,128)S(1)}, f32[2,48,8,128]{3,2,1,0:T(8,128)S(1)}, u32[]{:S(2)}, u32[]{:S(2)}) collective-permute-start(f32[2,48,8,128]{3,2,1,0:T(8,128)S(1)} %get-tuple-element.18), channel_id=1, source_target_pairs={{0,4},{4,0},{1,5},{5,1},{2,6},{6,2},{3,7},{7,3},{8,12},{12,8},{9,1... | collective-permute-start | bytes 1179656 | tf_op jit(solution)/shard_map/ppermute | solution.py:493
  9.9 10.2 %collective-permute-start.2 = (f32[2,128,128]{2,1,0:T(8,128)S(1)}, f32[2,128,128]{2,1,0:T(8,128)S(1)}, u32[]{:S(2)}, u32[]{:S(2)}) collective-permute-start(f32[2,128,128]{2,1,0:T(8,128)S(1)} %get-tuple-element.20), channel_id=1, source_target_pairs={{0,120},{8,0},{16,8},{24,16},{32,24},{40,32},{48,40},{56,48},{64,5... | collective-permute-start | bytes 393224 | tf_op jit(solution)/shard_map/ppermute | solution.py:495
  16.2 8.1 %collective-permute-start.1 = (f32[2,128,128]{2,1,0:T(8,128)S(1)}, f32[2,128,128]{2,1,0:T(8,128)S(1)}, u32[]{:S(2)}, u32[]{:S(2)}) collective-permute-start(f32[2,128,128]{2,1,0:T(8,128)S(1)} %get-tuple-element.20), channel_id=1, source_target_pairs={{0,8},{8,16},{16,24},{24,32},{32,40},{40,48},{48,56},{56,64},{64,7... | collective-permute-start | bytes 393224 | tf_op jit(solution)/shard_map/ppermute | solution.py:494
  32.4 2.0 %collective-permute-start.5 = (f32[8,128]{1,0:T(8,128)S(1)}, f32[8,128]{1,0:T(8,128)S(1)}, u32[]{:S(2)}, u32[]{:S(2)}) collective-permute-start(f32[8,128]{1,0:T(8,128)S(1)} %get-tuple-element.27), channel_id=1, source_target_pairs={{0,4},{4,0},{1,5},{5,1},{2,6},{6,2},{3,7},{7,3},{8,12},{12,8},{9,1... | collective-permute-start | bytes 12296 | tf_op jit(solution)/shard_map/ppermute | solution.py:480
  48.7 2.4 %collective-permute-start.6 = (f32[8,128]{1,0:T(8,128)S(1)}, f32[8,128]{1,0:T(8,128)S(1)}, u32[]{:S(2)}, u32[]{:S(2)}) collective-permute-start(f32[8,128]{1,0:T(8,128)S(1)} %reduce_sum.9.mine_ref), channel_id=1, source_target_pairs={{0,4},{4,0},{1,5},{5,1},{2,6},{6,2},{3,7},{7,3},{8,12},{12,8},{9,1... | collective-permute-start | bytes 12296 | tf_op jit(solution)/shard_map/ppermute | solution.py:484

commit v2 on v1

--- a/solution.py
+++ b/solution.py
@@ -38,13 +38,23 @@
     return pltpu.with_memory_space_constraint(array, pltpu.HBM)
 
 
-def vertical_faces_kernel(v_ref, head_ref, tail_ref, sems):
-    low = pltpu.make_async_copy(v_ref.at[0:2, :, pl.ds(0, NY)], head_ref, sems.at[0])
-    high = pltpu.make_async_copy(v_ref.at[0:2, :, pl.ds(ROWS - NY, NY)], tail_ref, sems.at[1])
-    low.start()
-    high.start()
-    low.wait()
-    high.wait()
+def vertical_faces_kernel(v_ref, one_ref, two_ref, sems):
+    odd = lax.axis_index("vert") % 2
+    high = ROWS - NY
+    part = S // 2
+    copies = []
+    for row, ref in (((1 - odd) * high, one_ref), (odd * high, two_ref)):
+        rows = pl.ds(pl.multiple_of(row, NY), NY)
+        for c in range(2):
+            for start in range(0, S, part):
+                snaps = pl.ds(start, part)
+                copies.append(
+                    pltpu.make_async_copy(v_ref.at[c, snaps, rows], ref.at[c, snaps], sems.at[len(copies)])
+                )
+    for copy in copies:
+        copy.start()
+    for copy in copies:
+        copy.wait()
 
 
 def vertical_faces(v):
@@ -55,7 +65,7 @@
         out_shape=(face, face),
         in_specs=[any_spec()],
         out_specs=(vmem_spec(), vmem_spec()),
-        scratch_shapes=[pltpu.SemaphoreType.DMA((2,))],
+        scratch_shapes=[pltpu.SemaphoreType.DMA((8,))],
         compiler_params=params(8),
     )(in_hbm(v))
 
@@ -113,33 +123,49 @@
     return lax.dot_general(left, right, NT, preferred_element_type=F32)
 
 
-def level(z):
-    return pl.ds(pl.multiple_of(z * NY, NY), NY)
+def level(s, z):
+    return slice(s * ROWS + z * NY, s * ROWS + (z + 1) * NY)
 
 
 def slope_z(v_ref, c, s, z):
-    return v_ref[c, s, level(z + 1), :] - v_ref[c, s, level(z - 1), :]
+    return v_ref[c, level(s, z + 1), :] - v_ref[c, level(s, z - 1), :]
 
 
 def slope_y(v_ref, hy_ref, c, s, z):
     row = lax.broadcasted_iota(jnp.int32, (NY, NX), 0)
     first = lax.axis_index("span") == 0
-    cells = v_ref[c, s, level(z), :]
-    face = hy_ref[c // 2, s, pl.ds(z, 1), :]
-    up = jnp.where(row == NY - 1, jnp.where(first, face, 0.0), pltpu.roll(cells, NY - 1, axis=0))
-    down = jnp.where(row == 0, jnp.where(first, 0.0, face), pltpu.roll(cells, 1, axis=0))
+    base = s * ROWS + z * NY
+
+    def rows(start):
+        inside = min(max(start, 0), S * ROWS - SUB)
+        part = v_ref[c, inside : inside + SUB, :]
+        return part if inside == start else pltpu.roll(part, (inside - start) % SUB, axis=0)
+
+    def shifted(by):
+        return jnp.concatenate([rows(base + by), rows(base + SUB + by)], axis=0)
+
+    face = hy_ref[c // 2, s, z : z + 1, :]
+    up = jnp.where(row == NY - 1, jnp.where(first, face, 0.0), shifted(1))
+    down = jnp.where(row == 0, jnp.where(first, 0.0, face), shifted(-1))
     return up - down
 
 
-def slope_x(v_ref, edge_ref, c, s, z):
-    lane = lax.broadcasted_iota(jnp.int32, (NY, NX), 1)
-    cells = v_ref[c, s, level(z), :]
-    edge = edge_ref[c - 1, level(z), :]
+def lanes():
+    return lax.broadcasted_iota(jnp.int32, (NY, NX), 1)
+
+
+def inner_slope_x(v_ref, c, s, z):
+    cells = v_ref[c, level(s, z), :]
+    up = jnp.where(lanes() == NX - 1, 0.0, pltpu.roll(cells, NX - 1, axis=1))
+    down = jnp.where(lanes() == 0, 0.0, pltpu.roll(cells, 1, axis=1))
+    return up - down
+
+
+def edge_slope_x(edge_ref, k, s, z):
+    edge = edge_ref[k, level(0, z), :]
     if s:
         edge = pltpu.roll(edge, NX - 2 * s, axis=1)
-    up = jnp.where(lane == NX - 1, edge, pltpu.roll(cells, NX - 1, axis=1))
-    down = jnp.where(lane == 0, edge, pltpu.roll(cells, 1, axis=1))
-    return up - down
+    return jnp.where((lanes() == 0) | (lanes() == NX - 1), edge, 0.0)
 
 
 def send_out(places, scratch, refs, sems):
@@ -153,108 +179,132 @@
         pltpu.make_async_copy(a, b, sems.at[i]).wait()
 
 
-def first_kernel(v_ref, hy_ref, h_out, l_out, part_ref, acc_ref, h_ref, l_ref, sems):
+def first_kernel(v_ref, hy_ref, h_out, l_out, part_ref, wx_ref, acc_ref, h_ref, l_ref, sems):
     def vorticity(z):
         for s in range(0, S, 2):
             pair = (0.5 * (slope_y(v_ref, hy_ref, 2, t, z) - slope_z(v_ref, 1, t, z)) for t in (s, s + 1))
             split_store(*pair, s // 2, z - 1, h_ref, l_ref)
         send_out([z - 1], (h_ref, l_ref), (h_out, l_out), sems)
 
-    def step(z, carry):
+    def slopes(z):
+        for s in range(S):
+            wx_ref[level(s, z), :] = inner_slope_x(v_ref, 2, s, z)
+
+    vorticity(1)
+    slopes(0)
+    slopes(1)
+    vorticity(2)
+    slopes(2)
+    acc_ref[...] = products(h_ref, l_ref, [0])
+    for z in range(3, NZ - 1):
+        vorticity(z)
+        slopes(z)
         acc_ref[...] += products(h_ref, l_ref, [z - 2])
-        vorticity(z)
-        return carry
-
-    acc_ref[...] = jnp.zeros_like(acc_ref)
-    vorticity(1)
-    lax.fori_loop(2, NZ - 1, step, 0)
-    acc_ref[...] += products(h_ref, l_ref, [NZ - 3])
-
-    def outer(k, carry):
+    for k in range(2):
         for s in range(S):
             part_ref[k, s] = slope_y(v_ref, hy_ref, 2, s, k * (NZ - 1))
-        return carry
-
-    lax.fori_loop(0, 2, outer, 0)
-    wait_out((h_ref, l_ref), (h_out, l_out), sems)
-
+    slopes(NZ - 1)
+    acc_ref[...] += products(h_ref, l_ref, [NZ - 3])
+
+    @pl.when(lax.axis_index("span") >= 0)
+    def _():
+        wait_out((h_ref, l_ref), (h_out, l_out), sems)
 
 def first_component(block, hy):
+    block = block.reshape(3, S * ROWS, NX)
     half = pltpu.HBM((6, R, PAIR), BF16)
     return pl.pallas_call(
         first_kernel,
         name="first_component",
-        out_shape=(half, half, pltpu.VMEM((2, S, NY, NX), F32), pltpu.VMEM((R, R), F32)),
+        out_shape=(
+            half,
+            half,
+            pltpu.VMEM((2, S, NY, NX), F32),
+            pltpu.VMEM((S * ROWS, NX), F32),
+            pltpu.VMEM((R, R), F32),
+        ),
         in_specs=[vmem_spec()] * 2,
-        out_specs=(any_spec(), any_spec(), vmem_spec(), vmem_spec()),
+        out_specs=(any_spec(), any_spec(), vmem_spec(), vmem_spec(), vmem_spec()),
         scratch_shapes=[pltpu.VMEM((6, R, PAIR), BF16)] * 2 + [pltpu.SemaphoreType.DMA((2,))],
         compiler_params=params(8),
         cost_estimate=pl.CostEstimate(flops=4 * R * R * 6 * PAIR, bytes_accessed=6 * MIB, transcendentals=0),
     )(*in_vmem(block, hy))
 
 
-def rest_kernel(v_ref, hy_ref, left_ref, right_ref, old_ref, h_out, l_out, part_ref, acc_ref, edge_ref, h_ref, l_ref, sems):
-    lane = lax.broadcasted_iota(jnp.int32, (NY, NX), 1)
+def rest_kernel(
+    v_ref, hy_ref, even_ref, odd_ref, wx_ref, old_ref, h_out, l_out, part_ref, acc_ref, h_last, l_last,
+    edge_ref, h_ref, l_ref, sems
+):
+    lane = lanes()
     stream = lax.axis_index("stream")
+    even = stream % 2 == 0
     for c in range(2):
         for z in range(NZ):
             rows = pl.ds(z * NY, NY)
-            before = jnp.where(stream > 0, left_ref[c, rows, :], 0.0)
-            behind = jnp.where(stream < lax.axis_size("stream") - 1, right_ref[c, rows, :], 0.0)
-            edge_ref[c, rows, :] = jnp.where(lane % 2 == 0, before, pltpu.roll(behind, NX - 2, axis=1))
+            one, two = even_ref[c, rows, :], odd_ref[c, rows, :]
+            left, right = jnp.where(even, two, one), jnp.where(even, one, two)
+            before = jnp.where(stream > 0, left, 0.0)
+            behind = jnp.where(stream < lax.axis_size("stream") - 1, right, 0.0)
+            edge_ref[c, rows, :] = jnp.where(lane % 2 == 0, -before, pltpu.roll(behind, NX - 2, axis=1))
+
+    def slope_wx(s, z):
+        return wx_ref[level(s, z), :] + edge_slope_x(edge_ref, 1, s, z)
 
     def second(z):
         for s in range(0, S, 2):
-            pair = (0.5 * (slope_z(v_ref, 0, t, z) - slope_x(v_ref, edge_ref, 2, t, z)) for t in (s, s + 1))
+            pair = (0.5 * (slope_z(v_ref, 0, t, z) - slope_wx(t, z)) for t in (s, s + 1))
             split_store(*pair, s // 2, z - 1, h_ref, l_ref)
         send_out([z - 1], (h_ref, l_ref), (h_out, l_out), sems)
 
     def third(z):
         for s in range(0, S, 2):
             pair = (
-                0.5 * (slope_x(v_ref, edge_ref, 1, t, z) - slope_y(v_ref, hy_ref, 0, t, z)) for t in (s, s + 1)
+                0.5
+                * (inner_slope_x(v_ref, 1, t, z) + edge_slope_x(edge_ref, 0, t, z) - slope_y(v_ref, hy_ref, 0, t, z))
+                for t in (s, s + 1)
             )
-            split_store(*pair, s // 2, z + 6, h_ref, l_ref)
-        send_out([z + 6], (h_ref, l_ref), (h_out, l_out), sems)
-
-    def step(z, carry):
-        acc_ref[...] += products(h_ref, l_ref, [z - 2, z + 5])
+            if z < NZ - 2:
+                split_store(*pair, s // 2, z + 6, h_ref, l_ref)
+            else:
+                split_store(*pair, s // 2, z - NZ + 2, h_last, l_last)
+        if z < NZ - 2:
+            send_out([z + 6], (h_ref, l_ref), (h_out, l_out), sems)
+
+    third(0)
+    second(1)
+    third(1)
+    acc_ref[...] = old_ref[...] + products(h_ref, l_ref, [6])
+    for z in range(2, NZ - 1):
         second(z)
         third(z)
-        return carry
-
-    third(0)
-    acc_ref[...] = old_ref[...] + products(h_ref, l_ref, [6])
-    second(1)
-    third(1)
-    lax.fori_loop(2, NZ - 1, step, 0)
-    acc_ref[...] += products(h_ref, l_ref, [NZ - 3, NZ + 4])
+        acc_ref[...] += products(h_ref, l_ref, [z - 2, z + 5])
     third(NZ - 1)
-    acc_ref[...] += products(h_ref, l_ref, [NZ + 5])
-
-    def outer(k, carry):
+    acc_ref[...] += products(h_ref, l_ref, [NZ - 3])
+    for k in range(2):
         for s in range(S):
-            part_ref[k, s] = slope_x(v_ref, edge_ref, 2, s, k * (NZ - 1))
-        return carry
-
-    lax.fori_loop(0, 2, outer, 0)
-    wait_out((h_ref, l_ref), (h_out, l_out), sems)
-
-
-def other_components(block, hy, left, right, acc):
-    half = pltpu.HBM((14, R, PAIR), BF16)
+            part_ref[k, s] = slope_wx(s, k * (NZ - 1))
+    acc_ref[...] += products(h_last, l_last, range(2))
+
+    @pl.when(stream >= 0)
+    def _():
+        wait_out((h_ref, l_ref), (h_out, l_out), sems)
+
+
+def other_components(block, hy, even, odd, wx, acc):
+    block = block.reshape(3, S * ROWS, NX)
+    half, last = pltpu.HBM((12, R, PAIR), BF16), pltpu.VMEM((2, R, PAIR), BF16)
     return pl.pallas_call(
         rest_kernel,
         name="other_components",
-        out_shape=(half, half, pltpu.VMEM((2, S, NY, NX), F32), pltpu.VMEM((R, R), F32)),
-        in_specs=[vmem_spec()] * 5,
-        out_specs=(any_spec(), any_spec(), vmem_spec(), vmem_spec()),
+        out_shape=(half, half, pltpu.VMEM((2, S, NY, NX), F32), pltpu.VMEM((R, R), F32), last, last),
+        in_specs=[vmem_spec()] * 6,
+        out_specs=(any_spec(), any_spec()) + (vmem_spec(),) * 4,
         scratch_shapes=[pltpu.VMEM((2, ROWS, NX), F32)]
-        + [pltpu.VMEM((14, R, PAIR), BF16)] * 2
+        + [pltpu.VMEM((12, R, PAIR), BF16)] * 2
         + [pltpu.SemaphoreType.DMA((2,))],
         compiler_params=params(12),
         cost_estimate=pl.CostEstimate(flops=4 * R * R * 14 * PAIR, bytes_accessed=12 * MIB, transcendentals=0),
-    )(*in_vmem(block, hy, left, right, acc))
+    )(*in_vmem(block, hy, even, odd, wx, acc))
 
 
 def lane_fold():
@@ -268,27 +318,38 @@
 
 
 def boundary_kernel(
-    v_ref, wy_ref, wx_ref, below_ref, above_ref, acc_ref, h_ref, l_ref, mine_ref, other_ref
+    v_ref, wy_ref, wx_ref, one_ref, two_ref, acc_ref, h_ref, l_ref, mine_ref, other_ref, sum_ref
 ):
     vert = lax.axis_index("vert")
     has_below, has_above = vert > 0, vert < lax.axis_size("vert") - 1
 
-    def dz(c, s, k):
-        if k:
-            return jnp.where(has_above, above_ref[c, s], 0.0) - v_ref[c, s, pl.ds((NZ - 2) * NY, NY), :]
-        return v_ref[c, s, pl.ds(NY, NY), :] - jnp.where(has_below, below_ref[c, s], 0.0)
-
-    for k in range(2):
-        for s in range(0, S, 2):
-            split_store(
-                *(0.5 * (wy_ref[k, t] - dz(1, t, k)) for t in (s, s + 1)),
-                s // 2, k, h_ref, l_ref,
-            )
-            split_store(
-                *(0.5 * (dz(0, t, k) - wx_ref[k, t]) for t in (s, s + 1)),
-                s // 2, 2 + k, h_ref, l_ref,
-            )
-    total = acc_ref[...] + products(h_ref, l_ref, range(4))
+    def vorticity(below_ref, above_ref):
+        def dz(c, s, k):
+            if k:
+                return jnp.where(has_above, above_ref[c, s], 0.0) - v_ref[c, s, pl.ds((NZ - 2) * NY, NY), :]
+            return v_ref[c, s, pl.ds(NY, NY), :] - jnp.where(has_below, below_ref[c, s], 0.0)
+
+        for k in range(2):
+            for s in range(0, S, 2):
+                first = (0.5 * (wy_ref[k, t] - dz(1, t, k)) for t in (s, s + 1))
+                split_store(*first, s // 2, k, h_ref, l_ref)
+        for k in range(2):
+            for s in range(0, S, 2):
+                second = (0.5 * (dz(0, t, k) - wx_ref[k, t]) for t in (s, s + 1))
+                split_store(*second, s // 2, 2 + k, h_ref, l_ref)
+            if not k:
+                sum_ref[...] = acc_ref[...] + products(h_ref, l_ref, range(2))
+        sum_ref[...] += products(h_ref, l_ref, range(2, 4))
+
+    @pl.when(vert % 2 == 0)
+    def _():
+        vorticity(two_ref, one_ref)
+
+    @pl.when(vert % 2 == 1)
+    def _():
+        vorticity(one_ref, two_ref)
+
+    total = sum_ref[...]
     total = jnp.where(same_cell(), total, 0.0).reshape(S, SUB, R).sum(1)
     total = lax.dot_general(
         total, lane_fold(), (((1,), (0,)), ((), ())), precision=HIGH, preferred_element_type=F32
@@ -305,7 +366,7 @@
     other_ref[...] = jnp.where(first, bottom, top)
 
 
-def boundary(block, wy, wx, below, above, acc):
+def boundary(block, wy, wx, one, two, acc):
     half = pltpu.VMEM((4, R, PAIR), BF16)
     sums = pltpu.VMEM((SUB, NX), F32)
     return pl.pallas_call(
@@ -314,8 +375,9 @@
         out_shape=(half, half, sums, sums),
         in_specs=[vmem_spec()] * 6,
         out_specs=(vmem_spec(),) * 4,
+        scratch_shapes=[pltpu.VMEM((R, R), F32)],
         compiler_params=params(8),
-    )(*in_vmem(block, wy, wx, below, above, acc))
+    )(*in_vmem(block, wy, wx, one, two, acc))
 
 
 def eliminate(work):
@@ -348,7 +410,7 @@
     return work
 
 
-def modes_kernel(count, mine_ref, other_ref, edge_h_ref, edge_l_ref, *refs):
+def modes_kernel(count, mine_ref, other_ref, edge_h_ref, edge_l_ref, last_h_ref, last_l_ref, *refs):
     parts, (out_ref, factor_ref, h_ref, l_ref, wide_ref, corner_ref, buffer, sems, in_sems) = refs[:4], refs[4:]
     loads, start = [], 0
     for k in range(2):
@@ -404,30 +466,34 @@
 
     slots = buffer.shape[0]
 
-    group = 4
+    group = 6
 
     def copy_out(place):
         q = place - group
         c = jnp.where(q < 0, place // 2, jnp.where(q < 6, 0, jnp.where(q < 12, 1, 2)))
-        z = jnp.where(q < 0, place % 2 * (NZ - 1), jnp.where(q < 12, q % 6 + 1, q - 12))
+        z = jnp.where(place < 4, place % 2 * (NZ - 1), jnp.where(q < 0, place + 2, jnp.where(q < 12, q % 6 + 1, q - 12)))
         slot = place % slots
         return pltpu.make_async_copy(buffer.at[slot], out_ref.at[c, :, z], sems.at[slot])
+
+    def held(k):
+        if k < 4:
+            return edge_h_ref[k], edge_l_ref[k]
+        return last_h_ref[k - 4], last_l_ref[k - 4]
 
     def apply(step, carry, source=None):
         first = step * group
         if source is None:
-            source = (h_ref, l_ref)
-            start = first - group
 
             @pl.when(step >= slots // group)
             def _():
                 for k in range(group):
                     copy_out(first + k - slots).wait()
-        else:
-            start = 0
+
+            def source(k):
+                return h_ref[first - group + k], l_ref[first - group + k]
 
         for k in range(group):
-            h, l = (ref[start + k] for ref in source)
+            h, l = source(k)
             part = jnp.dot(
                 wide_ref[...], jnp.concatenate([h[:cut], h[:cut], l[:cut]], axis=0), preferred_element_type=F32
             )
@@ -440,12 +506,11 @@
                 for half in range(2):
                     tile = value[:, half * NX : (half + 1) * NX].reshape(rows, SUB, NX)
                     buffer[(first + k) % slots, low : low + rows, half * SUB : (half + 1) * SUB, :] = tile
-        for k in range(group):
             copy_out(first + k).start()
         return carry
 
-    lax.fori_loop(0, 1, lambda step, carry: apply(0, carry, (edge_h_ref, edge_l_ref)), 0)
-    for pair, low, high in zip(loads, (1, 2), (2, 6)):
+    lax.fori_loop(0, 1, lambda step, carry: apply(0, carry, held), 0)
+    for pair, low, high in zip(loads, (1, 2), (2, 4)):
         for load in pair:
             load.wait()
         lax.fori_loop(low, high, apply, 0)
@@ -453,7 +518,7 @@
         copy_out(place).wait()
 
 
-def modes_and_factor(mine, other, edge_halves, halves, count):
+def modes_and_factor(mine, other, held, halves, count):
     return pl.pallas_call(
         functools.partial(modes_kernel, count),
         name="modes",
@@ -461,18 +526,24 @@
             pltpu.HBM((3, S, NZ, NY, NX), F32),
             jax.ShapeDtypeStruct((S, S), F32),
         ),
-        in_specs=[vmem_spec()] * 4 + [any_spec()] * 4,
+        in_specs=[vmem_spec()] * 6 + [any_spec()] * 4,
         out_specs=(any_spec(), vmem_spec()),
-        scratch_shapes=[pltpu.VMEM((20, R, PAIR), BF16)] * 2
+        scratch_shapes=[pltpu.VMEM((18, R, PAIR), BF16)] * 2
         + [pltpu.VMEM((R, 6 * NX), BF16), pltpu.VMEM((2 * NX, 2 * NX), BF16)]
         + [pltpu.VMEM((12, S, NY, NX), F32), pltpu.SemaphoreType.DMA((12,)), pltpu.SemaphoreType.DMA((4,))],
         compiler_params=params(24),
-    )(*in_vmem(mine, other, *edge_halves), *(in_hbm(h) for h in halves))
+    )(*in_vmem(mine, other, *held), *(in_hbm(h) for h in halves))
 
 
 def ring(axis, shift):
     count = lax.axis_size(axis)
     return [(i, (i + shift) % count) for i in range(count)]
+
+
+def neighbours(axis, first):
+    count = lax.axis_size(axis)
+    pairs = [(i, (i + 1) % count) for i in range(first, count, 2)]
+    return pairs + [(b, a) for a, b in pairs]
 
 
 def total_over_devices(mine, other):
@@ -486,20 +557,22 @@
 
 def per_device(velocity):
     v = velocity.reshape(3, S, ROWS, NX)
-    head, tail = vertical_faces(v)
-    below = lax.ppermute(tail, "vert", ring("vert", 1))
-    above = lax.ppermute(head, "vert", ring("vert", -1))
+    one, two = vertical_faces(v)
+    one = lax.ppermute(one, "vert", neighbours("vert", 0))
+    two = lax.ppermute(two, "vert", neighbours("vert", 1))
     xs, ys = side_faces(v)
     hy = lax.ppermute(ys, "span", ring("span", 1))
-    left = lax.ppermute(xs, "stream", ring("stream", 1))
-    right = lax.ppermute(xs, "stream", ring("stream", -1))
-    *head_halves, wy, acc = first_component(v, hy)
-    *rest_halves, wx, acc = other_components(v, hy, left, right, acc)
-    *edge_halves, mine, other = boundary(v, wy, wx, below, above, acc)
+    even = lax.ppermute(xs, "stream", neighbours("stream", 0))
+    odd = lax.ppermute(xs, "stream", neighbours("stream", 1))
+    *head_halves, wy, wx, acc = first_component(v, hy)
+    *rest_halves, wx, acc, last_high, last_low = other_components(v, hy, even, odd, wx, acc)
+    *edge_halves, mine, other = boundary(v, wy, wx, one, two, acc)
     mine, other = total_over_devices(mine, other)
     devices = lax.axis_size("stream") * lax.axis_size("span") * lax.axis_size("vert")
     count = float(3 * NZ * NY * NX * devices)
-    return modes_and_factor(mine, other, edge_halves, head_halves + rest_halves, count)
+    return modes_and_factor(
+        mine, other, edge_halves + [last_high, last_low], head_halves + rest_halves, count
+    )
 
 
 def solution(mesh):

time: 60.9 us -> 60.3 us (level)
  blocking collectives: 14.1 us -> 18.6 us
  Pallas kernels: 26 us -> 22.4 us
  waiting for transfers between devices: 5.84 us -> 3.79 us
    all_to_all x1, blocking collectives: 14.1 us -> 18.6 us  [total_over_devices(): lax.all_to_all(jnp.broadcast_to(mine, (peers,) + mine.shape), axes, 0, 0)]
    ppermute x4, waiting for transfers between devices: 4.19 us -> 2.14 us  [the longest x1 1.18 us: per_device(): odd = lax.ppermute(xs, 'stream', neighbours('stream', 1))]
    pallas_call x1, Pallas kernels: 6.36 us -> 4.4 us  [other_components(): pl.pallas_call(rest_kernel, name='other_components', out_shape=(half, hal...]
    pallas_call x1, Pallas kernels: 3.85 us -> 2.57 us  [first_component(): pl.pallas_call(first_kernel, name='first_component', out_shape=(half, hal...]
  transfers between devices with their start and end apart: 7 -> 7, of which waited for: 3 -> 4; matrix products, arithmetic and copies ran while one was open for 0% -> 0% of each run, Pallas kernels for 22% -> 16%
where the time goes in v2:
time: 60.3 us; the launch traced here: 60.2 us
  Pallas kernels  22.4 us (37%)
  blocking collectives  18.6 us (31%)
  starting transfers between devices  14.5 us (24%)
  waiting for transfers between devices  3.79 us (6%)
  between operations  0.86 us (1%)
    all_to_all x1, blocking collectives, total_over_devices(): lax.all_to_all(jnp.broadcast_to(mine, (peers,) + mine.shape), axes, 0, 0)  18.6 us
    pallas_call x1, Pallas kernels, modes_and_factor(): pl.pallas_call(functools.partial(modes_kernel, count), name='modes', out_...  9.08 us
    ppermute x1, starting transfers between devices, per_device(): odd = lax.ppermute(xs, 'stream', neighbours('stream', 1))  6.22 us
    pallas_call x1, Pallas kernels, other_components(): pl.pallas_call(rest_kernel, name='other_components', out_shape=(half, hal...  4.4 us
    pallas_call x1, Pallas kernels, side_faces(): pl.pallas_call(side_faces_kernel, name='side_faces', out_shape=(pltpu.VME...  2.93 us
    pallas_call x1, Pallas kernels, first_component(): pl.pallas_call(first_kernel, name='first_component', out_shape=(half, hal...  2.57 us
    ppermute x1, starting transfers between devices, per_device(): one = lax.ppermute(one, 'vert', neighbours('vert', 0))  2.12 us
    ppermute x1, starting transfers between devices, per_device(): two = lax.ppermute(two, 'vert', neighbours('vert', 1))  1.82 us
  transfers between devices with their start and end apart: 7, of which 4 were waited for; matrix products, arithmetic and copies ran while one was open for 0% of the time, Pallas kernels for 16%

profile of v2, /device:TPU:1, one launch (start us, length us, event | category | flops | bytes accessed | tf_op | source)
XLA Modules:
  0.0 60.2 jit_solution(14833161303632315235)
XLA Ops:
  0.6 0.0 copy-start
  0.6 1.7 %vertical_faces.1 = (f32[2,48,16,128]{3,2,1,0:T(8,128)S(1)}, f32[2,48,16,128]{3,2,1,0:T(8,128)S(1)}) custom-call(f32[3,48,128,128]{3,2,1,0:T(8,128)} %bitcast.2), custom_call_target="tpu_custom_call" | custom-call | tf_op jit(solution)/shard_map/vertical_faces/pallas_call | solution.py:62
  2.3 2.1 %collective-permute-start.3 = (f32[2,48,16,128]{3,2,1,0:T(8,128)S(1)}, f32[2,48,16,128]{3,2,1,0:T(8,128)S(1)}, u32[]{:S(2)}, u32[]{:S(2)}) collective-permute-start(f32[2,48,16,128]{3,2,1,0:T(8,128)S(1)} %get-tuple-element.27), channel_id=1, source_target_pairs={{0,1},{2,3},{1,0},{3,2},{4,5},{6,7},{5,4},{7,6},{8,9},{10,11},{9,8... | collective-permute-start | bytes 2359304 | tf_op jit(solution)/shard_map/ppermute | solution.py:561
  4.5 1.8 %collective-permute-start.4 = (f32[2,48,16,128]{3,2,1,0:T(8,128)S(1)}, f32[2,48,16,128]{3,2,1,0:T(8,128)S(1)}, u32[]{:S(2)}, u32[]{:S(2)}) collective-permute-start(f32[2,48,16,128]{3,2,1,0:T(8,128)S(1)} %get-tuple-element.28), channel_id=1, source_target_pairs={{1,2},{3,0},{2,1},{0,3},{5,6},{7,4},{6,5},{4,7},{9,10},{11,8},{10,... | collective-permute-start | bytes 2359304 | tf_op jit(solution)/shard_map/ppermute | solution.py:562
  6.3 0.0 copy-done
  6.3 2.9 %side_faces.1 = (f32[2,128,128]{2,1,0:T(8,128)S(1)}, f32[2,48,8,128]{3,2,1,0:T(8,128)S(1)}) custom-call(f32[3,48,128,128]{3,2,1,0:T(8,128)S(1)} %bitcast.3), custom_call_target="tpu_custom_call" | custom-call | tf_op jit(solution)/shard_map/side_faces/pallas_call | solution.py:96
  9.2 1.3 %collective-permute-start = (f32[2,48,8,128]{3,2,1,0:T(8,128)S(1)}, f32[2,48,8,128]{3,2,1,0:T(8,128)S(1)}, u32[]{:S(2)}, u32[]{:S(2)}) collective-permute-start(f32[2,48,8,128]{3,2,1,0:T(8,128)S(1)} %get-tuple-element.21), channel_id=1, source_target_pairs={{0,4},{4,0},{1,5},{5,1},{2,6},{6,2},{3,7},{7,3},{8,12},{12,8},{9,1... | collective-permute-start | bytes 1179656 | tf_op jit(solution)/shard_map/ppermute | solution.py:564
  10.5 6.2 %collective-permute-start.2 = (f32[2,128,128]{2,1,0:T(8,128)S(1)}, f32[2,128,128]{2,1,0:T(8,128)S(1)}, u32[]{:S(2)}, u32[]{:S(2)}) collective-permute-start(f32[2,128,128]{2,1,0:T(8,128)S(1)} %get-tuple-element.23), channel_id=1, source_target_pairs={{8,16},{24,32},{40,48},{56,64},{72,80},{88,96},{104,112},{120,0},{... | collective-permute-start | bytes 393224 | tf_op jit(solution)/shard_map/ppermute | solution.py:566
  16.8 0.0 collective-permute-start.1
  16.8 0.0 collective-permute-done.hy_ref
  16.8 2.6 %first_component.1 = (bf16[6,384,256]{2,1,0:T(8,128)(2,1)}, bf16[6,384,256]{2,1,0:T(8,128)(2,1)}, f32[2,48,16,128]{3,2,1,0:T(8,128)S(1)}, f32[6144,128]{1,0:T(8,128)S(1)}, f32[384,384]{1,0:T(8,128)S(1)}) custom-call(f32[3,6144,128]{2,1,0:T(8,128)S(1)} %bitcast.4, f32[2,48,8,128]{3,2,1,0:T(8,128)S(1)} %collective-permute-done.hy_ref), custom_call_target="tpu_custom_call" | custom-call | flops 905969664 | bytes 6291456 | tf_op jit(solution)/shard_map/first_component/pallas_call | solution.py:216
  19.3 1.2 %collective-permute-done.2.odd_ref = f32[2,128,128]{2,1,0:T(8,128)S(1)} collective-permute-done((f32[2,128,128]{2,1,0:T(8,128)S(1)}, f32[2,128,128]{2,1,0:T(8,128)S(1)}, u32[]{:S(2)}, u32[]{:S(2)}) %collective-permute-start.2) | collective-permute-done | bytes 131104 | tf_op jit(solution)/shard_map/ppermute | solution.py:566
  20.5 1.0 %collective-permute-done.1.even_ref = f32[2,128,128]{2,1,0:T(8,128)S(1)} collective-permute-done((f32[2,128,128]{2,1,0:T(8,128)S(1)}, f32[2,128,128]{2,1,0:T(8,128)S(1)}, u32[]{:S(2)}, u32[]{:S(2)}) %collective-permute-start.1) | collective-permute-done | bytes 131104 | tf_op jit(solution)/shard_map/ppermute | solution.py:565
  21.5 4.4 %other_components.1 = (bf16[12,384,256]{2,1,0:T(8,128)(2,1)}, bf16[12,384,256]{2,1,0:T(8,128)(2,1)}, f32[2,48,16,128]{3,2,1,0:T(8,128)S(1)}, f32[384,384]{1,0:T(...) custom-call(f32[3,6144,128]{2,1,0:T(8,128)S(1)} %bitcast.5, ...), custom_call_target="tpu_custom_call" | custom-call | flops 2113929216 | bytes 12582912 | tf_op jit(solution)/shard_map/other_components/pallas_call | solution.py:296
  25.9 0.0 collective-permute-done.3.one_ref
  25.9 0.0 collective-permute-done.4.two_ref
  25.9 1.7 %boundary.1 = (bf16[4,384,256]{2,1,0:T(8,128)(2,1)S(1)}, bf16[4,384,256]{2,1,0:T(8,128)(2,1)S(1)}, f32[8,128]{1,0:T(8,128)S(1)}, f32[8,128]{1,0:T(8,128)S(1)}) custom-call(f32[3,48,128,128]{3,2,1,0:T(8,128)S(1)} %bitcast.6, f32[2,48,16,128]{3,2,1,0:T(8,128)S(1)} %get-tuple-element.22.wy_ref, f32[2,48,16,128]{3,2,1,0:T(8,128)S(1)} %get-tuple-element.26.wx_ref, ...), custom_call_target="tpu_custom_call" | custom-call | tf_op jit(solution)/shard_map/boundary/pallas_call | solution.py:372
  27.6 1.2 %collective-permute-start.5 = (f32[8,128]{1,0:T(8,128)S(1)}, f32[8,128]{1,0:T(8,128)S(1)}, u32[]{:S(2)}, u32[]{:S(2)}) collective-permute-start(f32[8,128]{1,0:T(8,128)S(1)} %get-tuple-element.31), channel_id=1, source_target_pairs={{0,4},{4,0},{1,5},{5,1},{2,6},{6,2},{3,7},{7,3},{8,12},{12,8},{9,1... | collective-permute-start | bytes 12296 | tf_op jit(solution)/shard_map/ppermute | solution.py:551
  28.8 0.8 %collective-permute-done.5 = f32[8,128]{1,0:T(8,128)S(1)} collective-permute-done((f32[8,128]{1,0:T(8,128)S(1)}, f32[8,128]{1,0:T(8,128)S(1)}, u32[]{:S(2)}, u32[]{:S(2)}) %collective-permute-start.5) | collective-permute-done | bytes 4128 | tf_op jit(solution)/shard_map/ppermute | solution.py:551
  29.7 18.6 %all_to_all.5 = f32[64,8,128]{2,1,0:T(8,128)S(1)} all-to-all(f32[64,8,128]{2,1,0:T(8,128)S(1)} %broadcast_in_dim.3), channel_id=1, replica_groups=mesh['stream'=16,'span'=2,'vert'=4] {'stream','vert'}, dimensions={0} | all-to-all | bytes 524288 | tf_op jit(solution)/shard_map/all_to_all | solution.py:554
  48.3 0.1 reduce_sum.9.mine_ref
  48.3 1.8 %collective-permute-start.6 = (f32[8,128]{1,0:T(8,128)S(1)}, f32[8,128]{1,0:T(8,128)S(1)}, u32[]{:S(2)}, u32[]{:S(2)}) collective-permute-start(f32[8,128]{1,0:T(8,128)S(1)} %reduce_sum.9.mine_ref), channel_id=1, source_target_pairs={{0,4},{4,0},{1,5},{5,1},{2,6},{6,2},{3,7},{7,3},{8,12},{12,8},{9,1... | collective-permute-start | bytes 12296 | tf_op jit(solution)/shard_map/ppermute | solution.py:555
  50.1 0.8 %collective-permute-done.6.other_ref = f32[8,128]{1,0:T(8,128)S(1)} collective-permute-done((f32[8,128]{1,0:T(8,128)S(1)}, f32[8,128]{1,0:T(8,128)S(1)}, u32[]{:S(2)}, u32[]{:S(2)}) %collective-permute-start.6) | collective-permute-done | bytes 4128 | tf_op jit(solution)/shard_map/ppermute | solution.py:555
  50.9 9.1 %modes.1 = (f32[3,48,8,16,128]{4,3,2,1,0:T(8,128)}, f32[48,48]{1,0:T(8,128)}) custom-call(f32[8,128]{1,0:T(8,128)S(1)} %reduce_sum.9.mine_ref, f32[8,128]{1,0:T(8,128)S(1)} %collective-permute-done.6.other_ref, bf16[4,384,256]{2,1,0:T(8,128)(2,1)S(1)} %get-tuple-element.32.edge_h_ref, bf16[4,384,256]{2,1,0:T(8,128)(2,1)S(1)} %get-tuple-element.33.edge_l_ref, ...), custom_call_target="tpu_custom_call" | custom-call | tf_op jit(solution)/shard_map/modes/pallas_call | solution.py:522
  (2 shorter events, 0.0 us)
Async XLA Ops:
  0.6 5.6 %copy-start = (f32[3,48,8,16,128]{4,3,2,1,0:T(8,128)S(1)}, f32[3,48,8,16,128]{4,3,2,1,0:T(8,128)}, u32[]{:S(2)}) copy-start(f32[3,48,8,16,128]{4,3,2,1,0:T(8,128)} %param.1) | copy-start | bytes 28311556
  2.3 23.5 %collective-permute-start.3 = (f32[2,48,16,128]{3,2,1,0:T(8,128)S(1)}, f32[2,48,16,128]{3,2,1,0:T(8,128)S(1)}, u32[]{:S(2)}, u32[]{:S(2)}) collective-permute-start(f32[2,48,16,128]{3,2,1,0:T(8,128)S(1)} %get-tuple-element.27), channel_id=1, source_target_pairs={{0,1},{2,3},{1,0},{3,2},{4,5},{6,7},{5,4},{7,6},{8,9},{10,11},{9,8... | collective-permute-start | bytes 2359304 | tf_op jit(solution)/shard_map/ppermute | solution.py:561
  4.5 21.4 %collective-permute-start.4 = (f32[2,48,16,128]{3,2,1,0:T(8,128)S(1)}, f32[2,48,16,128]{3,2,1,0:T(8,128)S(1)}, u32[]{:S(2)}, u32[]{:S(2)}) collective-permute-start(f32[2,48,16,128]{3,2,1,0:T(8,128)S(1)} %get-tuple-element.28), channel_id=1, source_target_pairs={{1,2},{3,0},{2,1},{0,3},{5,6},{7,4},{6,5},{4,7},{9,10},{11,8},{10,... | collective-permute-start | bytes 2359304 | tf_op jit(solution)/shard_map/ppermute | solution.py:562
  9.2 7.5 %collective-permute-start = (f32[2,48,8,128]{3,2,1,0:T(8,128)S(1)}, f32[2,48,8,128]{3,2,1,0:T(8,128)S(1)}, u32[]{:S(2)}, u32[]{:S(2)}) collective-permute-start(f32[2,48,8,128]{3,2,1,0:T(8,128)S(1)} %get-tuple-element.21), channel_id=1, source_target_pairs={{0,4},{4,0},{1,5},{5,1},{2,6},{6,2},{3,7},{7,3},{8,12},{12,8},{9,1... | collective-permute-start | bytes 1179656 | tf_op jit(solution)/shard_map/ppermute | solution.py:564
  10.5 10.0 %collective-permute-start.2 = (f32[2,128,128]{2,1,0:T(8,128)S(1)}, f32[2,128,128]{2,1,0:T(8,128)S(1)}, u32[]{:S(2)}, u32[]{:S(2)}) collective-permute-start(f32[2,128,128]{2,1,0:T(8,128)S(1)} %get-tuple-element.23), channel_id=1, source_target_pairs={{8,16},{24,32},{40,48},{56,64},{72,80},{88,96},{104,112},{120,0},{... | collective-permute-start | bytes 393224 | tf_op jit(solution)/shard_map/ppermute | solution.py:566
  16.8 4.7 %collective-permute-start.1 = (f32[2,128,128]{2,1,0:T(8,128)S(1)}, f32[2,128,128]{2,1,0:T(8,128)S(1)}, u32[]{:S(2)}, u32[]{:S(2)}) collective-permute-start(f32[2,128,128]{2,1,0:T(8,128)S(1)} %get-tuple-element.23), channel_id=1, source_target_pairs={{0,8},{16,24},{32,40},{48,56},{64,72},{80,88},{96,104},{112,120},{... | collective-permute-start | bytes 393224 | tf_op jit(solution)/shard_map/ppermute | solution.py:565
  27.6 2.0 %collective-permute-start.5 = (f32[8,128]{1,0:T(8,128)S(1)}, f32[8,128]{1,0:T(8,128)S(1)}, u32[]{:S(2)}, u32[]{:S(2)}) collective-permute-start(f32[8,128]{1,0:T(8,128)S(1)} %get-tuple-element.31), channel_id=1, source_target_pairs={{0,4},{4,0},{1,5},{5,1},{2,6},{6,2},{3,7},{7,3},{8,12},{12,8},{9,1... | collective-permute-start | bytes 12296 | tf_op jit(solution)/shard_map/ppermute | solution.py:551
  48.3 2.6 %collective-permute-start.6 = (f32[8,128]{1,0:T(8,128)S(1)}, f32[8,128]{1,0:T(8,128)S(1)}, u32[]{:S(2)}, u32[]{:S(2)}) collective-permute-start(f32[8,128]{1,0:T(8,128)S(1)} %reduce_sum.9.mine_ref), channel_id=1, source_target_pairs={{0,4},{4,0},{1,5},{5,1},{2,6},{6,2},{3,7},{7,3},{8,12},{12,8},{9,1... | collective-permute-start | bytes 12296 | tf_op jit(solution)/shard_map/ppermute | solution.py:555

commit v3 on v2

--- a/solution.py
+++ b/solution.py
@@ -470,30 +470,23 @@
 
     def copy_out(place):
         q = place - group
-        c = jnp.where(q < 0, place // 2, jnp.where(q < 6, 0, jnp.where(q < 12, 1, 2)))
-        z = jnp.where(place < 4, place % 2 * (NZ - 1), jnp.where(q < 0, place + 2, jnp.where(q < 12, q % 6 + 1, q - 12)))
-        slot = place % slots
-        return pltpu.make_async_copy(buffer.at[slot], out_ref.at[c, :, z], sems.at[slot])
-
-    def held(k):
-        if k < 4:
-            return edge_h_ref[k], edge_l_ref[k]
-        return last_h_ref[k - 4], last_l_ref[k - 4]
-
-    def apply(step, carry, source=None):
+        if q < 0:
+            c, z = place // 2, place % 2 * (NZ - 1) if place < 4 else place + 2
+        else:
+            c, z = q // 6, q % 6 + (q < 12)
+        return pltpu.make_async_copy(buffer.at[place], out_ref.at[c, :, z], sems.at[place])
+
+    def source(place):
+        if place < 4:
+            return edge_h_ref[place], edge_l_ref[place]
+        if place < group:
+            return last_h_ref[place - 4], last_l_ref[place - 4]
+        return h_ref[place - group], l_ref[place - group]
+
+    def apply(step):
         first = step * group
-        if source is None:
-
-            @pl.when(step >= slots // group)
-            def _():
-                for k in range(group):
-                    copy_out(first + k - slots).wait()
-
-            def source(k):
-                return h_ref[first - group + k], l_ref[first - group + k]
-
         for k in range(group):
-            h, l = source(k)
+            h, l = source(first + k)
             part = jnp.dot(
                 wide_ref[...], jnp.concatenate([h[:cut], h[:cut], l[:cut]], axis=0), preferred_element_type=F32
             )
@@ -505,16 +498,23 @@
                 rows = value.shape[0] // SUB
                 for half in range(2):
                     tile = value[:, half * NX : (half + 1) * NX].reshape(rows, SUB, NX)
-                    buffer[(first + k) % slots, low : low + rows, half * SUB : (half + 1) * SUB, :] = tile
+                    buffer[first + k, low : low + rows, half * SUB : (half + 1) * SUB, :] = tile
             copy_out(first + k).start()
-        return carry
-
-    lax.fori_loop(0, 1, lambda step, carry: apply(0, carry, held), 0)
-    for pair, low, high in zip(loads, (1, 2), (2, 4)):
+
+    @pl.when(lax.axis_index("stream") >= 0)
+    def _():
+        apply(0)
+
+    for pair in loads:
         for load in pair:
             load.wait()
-        lax.fori_loop(low, high, apply, 0)
-    for place in range(24 - slots, 24):
+
+    @pl.when(lax.axis_index("stream") >= 0)
+    def _():
+        for step in range(1, 4):
+            apply(step)
+
+    for place in range(slots):
         copy_out(place).wait()
 
 
@@ -530,8 +530,8 @@
         out_specs=(any_spec(), vmem_spec()),
         scratch_shapes=[pltpu.VMEM((18, R, PAIR), BF16)] * 2
         + [pltpu.VMEM((R, 6 * NX), BF16), pltpu.VMEM((2 * NX, 2 * NX), BF16)]
-        + [pltpu.VMEM((12, S, NY, NX), F32), pltpu.SemaphoreType.DMA((12,)), pltpu.SemaphoreType.DMA((4,))],
-        compiler_params=params(24),
+        + [pltpu.VMEM((24, S, NY, NX), F32), pltpu.SemaphoreType.DMA((24,)), pltpu.SemaphoreType.DMA((4,))],
+        compiler_params=params(32),
     )(*in_vmem(mine, other, *held), *(in_hbm(h) for h in halves))
 
 
@@ -558,6 +558,7 @@
 def per_device(velocity):
     v = velocity.reshape(3, S, ROWS, NX)
     one, two = vertical_faces(v)
+    v, one, two = lax.optimization_barrier((v, one, two))
     one = lax.ppermute(one, "vert", neighbours("vert", 0))
     two = lax.ppermute(two, "vert", neighbours("vert", 1))
     xs, ys = side_faces(v)

time: 60.3 us -> 59.8 us (level)
  transfers between devices with their start and end apart: 7 -> 7, of which waited for: 4 -> 4; matrix products, arithmetic and copies ran while one was open for 0% -> 0% of each run, Pallas kernels for 16% -> 17%
where the time goes in v3:
time: 59.8 us; the launch traced here: 59.7 us
  Pallas kernels  21.9 us (37%)
  blocking collectives  18.6 us (31%)
  starting transfers between devices  14.5 us (24%)
  waiting for transfers between devices  3.79 us (6%)
  between operations  0.86 us (1%)
    all_to_all x1, blocking collectives, total_over_devices(): lax.all_to_all(jnp.broadcast_to(mine, (peers,) + mine.shape), axes, 0, 0)  18.6 us
    pallas_call x1, Pallas kernels, modes_and_factor(): pl.pallas_call(functools.partial(modes_kernel, count), name='modes', out_...  8.56 us
    ppermute x1, starting transfers between devices, per_device(): odd = lax.ppermute(xs, 'stream', neighbours('stream', 1))  6.22 us
    pallas_call x1, Pallas kernels, other_components(): pl.pallas_call(rest_kernel, name='other_components', out_shape=(half, hal...  4.4 us
    pallas_call x1, Pallas kernels, side_faces(): pl.pallas_call(side_faces_kernel, name='side_faces', out_shape=(pltpu.VME...  2.93 us
    pallas_call x1, Pallas kernels, first_component(): pl.pallas_call(first_kernel, name='first_component', out_shape=(half, hal...  2.57 us
    ppermute x1, starting transfers between devices, per_device(): one = lax.ppermute(one, 'vert', neighbours('vert', 0))  2.12 us
    ppermute x1, starting transfers between devices, per_device(): two = lax.ppermute(two, 'vert', neighbours('vert', 1))  1.82 us
  transfers between devices with their start and end apart: 7, of which 4 were waited for; matrix products, arithmetic and copies ran while one was open for 0% of the time, Pallas kernels for 17%

profile of v3, /device:TPU:1, one launch (start us, length us, event | category | flops | bytes accessed | tf_op | source)
XLA Modules:
  0.0 59.7 jit_solution(17634504237197886277)
XLA Ops:
  0.6 0.0 copy-start
  0.6 1.7 %vertical_faces.1 = (f32[2,48,16,128]{3,2,1,0:T(8,128)S(1)}, f32[2,48,16,128]{3,2,1,0:T(8,128)S(1)}) custom-call(f32[3,48,128,128]{3,2,1,0:T(8,128)} %bitcast.2), custom_call_target="tpu_custom_call" | custom-call | tf_op jit(solution)/shard_map/vertical_faces/pallas_call | solution.py:62
  2.3 2.1 %collective-permute-start.3 = (f32[2,48,16,128]{3,2,1,0:T(8,128)S(1)}, f32[2,48,16,128]{3,2,1,0:T(8,128)S(1)}, u32[]{:S(2)}, u32[]{:S(2)}) collective-permute-start(f32[2,48,16,128]{3,2,1,0:T(8,128)S(1)} %get-tuple-element.33), channel_id=1, source_target_pairs={{0,1},{2,3},{1,0},{3,2},{4,5},{6,7},{5,4},{7,6},{8,9},{10,11},{9,8... | collective-permute-start | bytes 2359304 | tf_op jit(solution)/shard_map/ppermute | solution.py:562
  4.5 1.8 %collective-permute-start.4 = (f32[2,48,16,128]{3,2,1,0:T(8,128)S(1)}, f32[2,48,16,128]{3,2,1,0:T(8,128)S(1)}, u32[]{:S(2)}, u32[]{:S(2)}) collective-permute-start(f32[2,48,16,128]{3,2,1,0:T(8,128)S(1)} %get-tuple-element.34), channel_id=1, source_target_pairs={{1,2},{3,0},{2,1},{0,3},{5,6},{7,4},{6,5},{4,7},{9,10},{11,8},{10,... | collective-permute-start | bytes 2359304 | tf_op jit(solution)/shard_map/ppermute | solution.py:563
  6.3 0.0 copy-done
  6.3 2.9 %side_faces.1 = (f32[2,128,128]{2,1,0:T(8,128)S(1)}, f32[2,48,8,128]{3,2,1,0:T(8,128)S(1)}) custom-call(f32[3,48,128,128]{3,2,1,0:T(8,128)S(1)} %bitcast.3), custom_call_target="tpu_custom_call" | custom-call | tf_op jit(solution)/shard_map/side_faces/pallas_call | solution.py:96
  9.2 1.3 %collective-permute-start = (f32[2,48,8,128]{3,2,1,0:T(8,128)S(1)}, f32[2,48,8,128]{3,2,1,0:T(8,128)S(1)}, u32[]{:S(2)}, u32[]{:S(2)}) collective-permute-start(f32[2,48,8,128]{3,2,1,0:T(8,128)S(1)} %get-tuple-element.27), channel_id=1, source_target_pairs={{0,4},{4,0},{1,5},{5,1},{2,6},{6,2},{3,7},{7,3},{8,12},{12,8},{9,1... | collective-permute-start | bytes 1179656 | tf_op jit(solution)/shard_map/ppermute | solution.py:565
  10.5 6.2 %collective-permute-start.2 = (f32[2,128,128]{2,1,0:T(8,128)S(1)}, f32[2,128,128]{2,1,0:T(8,128)S(1)}, u32[]{:S(2)}, u32[]{:S(2)}) collective-permute-start(f32[2,128,128]{2,1,0:T(8,128)S(1)} %get-tuple-element.29), channel_id=1, source_target_pairs={{8,16},{24,32},{40,48},{56,64},{72,80},{88,96},{104,112},{120,0},{... | collective-permute-start | bytes 393224 | tf_op jit(solution)/shard_map/ppermute | solution.py:567
  16.8 0.0 collective-permute-start.1
  16.8 0.0 collective-permute-done.hy_ref
  16.8 2.6 %first_component.1 = (bf16[6,384,256]{2,1,0:T(8,128)(2,1)}, bf16[6,384,256]{2,1,0:T(8,128)(2,1)}, f32[2,48,16,128]{3,2,1,0:T(8,128)S(1)}, f32[6144,128]{1,0:T(8,128)S(1)}, f32[384,384]{1,0:T(8,128)S(1)}) custom-call(f32[3,6144,128]{2,1,0:T(8,128)S(1)} %bitcast.4, f32[2,48,8,128]{3,2,1,0:T(8,128)S(1)} %collective-permute-done.hy_ref), custom_call_target="tpu_custom_call" | custom-call | flops 905969664 | bytes 6291456 | tf_op jit(solution)/shard_map/first_component/pallas_call | solution.py:216
  19.3 1.2 %collective-permute-done.2.odd_ref = f32[2,128,128]{2,1,0:T(8,128)S(1)} collective-permute-done((f32[2,128,128]{2,1,0:T(8,128)S(1)}, f32[2,128,128]{2,1,0:T(8,128)S(1)}, u32[]{:S(2)}, u32[]{:S(2)}) %collective-permute-start.2) | collective-permute-done | bytes 131104 | tf_op jit(solution)/shard_map/ppermute | solution.py:567
  20.5 1.0 %collective-permute-done.1.even_ref = f32[2,128,128]{2,1,0:T(8,128)S(1)} collective-permute-done((f32[2,128,128]{2,1,0:T(8,128)S(1)}, f32[2,128,128]{2,1,0:T(8,128)S(1)}, u32[]{:S(2)}, u32[]{:S(2)}) %collective-permute-start.1) | collective-permute-done | bytes 131104 | tf_op jit(solution)/shard_map/ppermute | solution.py:566
  21.5 4.4 %other_components.1 = (bf16[12,384,256]{2,1,0:T(8,128)(2,1)}, bf16[12,384,256]{2,1,0:T(8,128)(2,1)}, f32[2,48,16,128]{3,2,1,0:T(8,128)S(1)}, f32[384,384]{1,0:T(...) custom-call(f32[3,6144,128]{2,1,0:T(8,128)S(1)} %bitcast.5, ...), custom_call_target="tpu_custom_call" | custom-call | flops 2113929216 | bytes 12582912 | tf_op jit(solution)/shard_map/other_components/pallas_call | solution.py:296
  25.9 0.0 collective-permute-done.3.one_ref
  25.9 0.0 collective-permute-done.4.two_ref
  25.9 1.7 %boundary.1 = (bf16[4,384,256]{2,1,0:T(8,128)(2,1)S(1)}, bf16[4,384,256]{2,1,0:T(8,128)(2,1)S(1)}, f32[8,128]{1,0:T(8,128)S(1)}, f32[8,128]{1,0:T(8,128)S(1)}) custom-call(f32[3,48,128,128]{3,2,1,0:T(8,128)S(1)} %bitcast.6, f32[2,48,16,128]{3,2,1,0:T(8,128)S(1)} %get-tuple-element.28.wy_ref, f32[2,48,16,128]{3,2,1,0:T(8,128)S(1)} %get-tuple-element.32.wx_ref, ...), custom_call_target="tpu_custom_call" | custom-call | tf_op jit(solution)/shard_map/boundary/pallas_call | solution.py:372
  27.6 1.2 %collective-permute-start.5 = (f32[8,128]{1,0:T(8,128)S(1)}, f32[8,128]{1,0:T(8,128)S(1)}, u32[]{:S(2)}, u32[]{:S(2)}) collective-permute-start(f32[8,128]{1,0:T(8,128)S(1)} %get-tuple-element.37), channel_id=1, source_target_pairs={{0,4},{4,0},{1,5},{5,1},{2,6},{6,2},{3,7},{7,3},{8,12},{12,8},{9,1... | collective-permute-start | bytes 12296 | tf_op jit(solution)/shard_map/ppermute | solution.py:551
  28.8 0.8 %collective-permute-done.5 = f32[8,128]{1,0:T(8,128)S(1)} collective-permute-done((f32[8,128]{1,0:T(8,128)S(1)}, f32[8,128]{1,0:T(8,128)S(1)}, u32[]{:S(2)}, u32[]{:S(2)}) %collective-permute-start.5) | collective-permute-done | bytes 4128 | tf_op jit(solution)/shard_map/ppermute | solution.py:551
  29.7 18.6 %all_to_all.5 = f32[64,8,128]{2,1,0:T(8,128)S(1)} all-to-all(f32[64,8,128]{2,1,0:T(8,128)S(1)} %broadcast_in_dim.3), channel_id=1, replica_groups=mesh['stream'=16,'span'=2,'vert'=4] {'stream','vert'}, dimensions={0} | all-to-all | bytes 524288 | tf_op jit(solution)/shard_map/all_to_all | solution.py:554
  48.3 0.1 reduce_sum.9.mine_ref
  48.3 1.8 %collective-permute-start.6 = (f32[8,128]{1,0:T(8,128)S(1)}, f32[8,128]{1,0:T(8,128)S(1)}, u32[]{:S(2)}, u32[]{:S(2)}) collective-permute-start(f32[8,128]{1,0:T(8,128)S(1)} %reduce_sum.9.mine_ref), channel_id=1, source_target_pairs={{0,4},{4,0},{1,5},{5,1},{2,6},{6,2},{3,7},{7,3},{8,12},{12,8},{9,1... | collective-permute-start | bytes 12296 | tf_op jit(solution)/shard_map/ppermute | solution.py:555
  50.1 0.8 %collective-permute-done.6.other_ref = f32[8,128]{1,0:T(8,128)S(1)} collective-permute-done((f32[8,128]{1,0:T(8,128)S(1)}, f32[8,128]{1,0:T(8,128)S(1)}, u32[]{:S(2)}, u32[]{:S(2)}) %collective-permute-start.6) | collective-permute-done | bytes 4128 | tf_op jit(solution)/shard_map/ppermute | solution.py:555
  50.9 8.6 %modes.1 = (f32[3,48,8,16,128]{4,3,2,1,0:T(8,128)}, f32[48,48]{1,0:T(8,128)}) custom-call(f32[8,128]{1,0:T(8,128)S(1)} %reduce_sum.9.mine_ref, f32[8,128]{1,0:T(8,128)S(1)} %collective-permute-done.6.other_ref, bf16[4,384,256]{2,1,0:T(8,128)(2,1)S(1)} %get-tuple-element.38.edge_h_ref, bf16[4,384,256]{2,1,0:T(8,128)(2,1)S(1)} %get-tuple-element.39.edge_l_ref, ...), custom_call_target="tpu_custom_call" | custom-call | tf_op jit(solution)/shard_map/modes/pallas_call | solution.py:522
  (2 shorter events, 0.0 us)
Async XLA Ops:
  0.6 5.6 %copy-start = (f32[3,48,8,16,128]{4,3,2,1,0:T(8,128)S(1)}, f32[3,48,8,16,128]{4,3,2,1,0:T(8,128)}, u32[]{:S(2)}) copy-start(f32[3,48,8,16,128]{4,3,2,1,0:T(8,128)} %param.1) | copy-start | bytes 28311556
  2.3 23.5 %collective-permute-start.3 = (f32[2,48,16,128]{3,2,1,0:T(8,128)S(1)}, f32[2,48,16,128]{3,2,1,0:T(8,128)S(1)}, u32[]{:S(2)}, u32[]{:S(2)}) collective-permute-start(f32[2,48,16,128]{3,2,1,0:T(8,128)S(1)} %get-tuple-element.33), channel_id=1, source_target_pairs={{0,1},{2,3},{1,0},{3,2},{4,5},{6,7},{5,4},{7,6},{8,9},{10,11},{9,8... | collective-permute-start | bytes 2359304 | tf_op jit(solution)/shard_map/ppermute | solution.py:562
  4.5 21.4 %collective-permute-start.4 = (f32[2,48,16,128]{3,2,1,0:T(8,128)S(1)}, f32[2,48,16,128]{3,2,1,0:T(8,128)S(1)}, u32[]{:S(2)}, u32[]{:S(2)}) collective-permute-start(f32[2,48,16,128]{3,2,1,0:T(8,128)S(1)} %get-tuple-element.34), channel_id=1, source_target_pairs={{1,2},{3,0},{2,1},{0,3},{5,6},{7,4},{6,5},{4,7},{9,10},{11,8},{10,... | collective-permute-start | bytes 2359304 | tf_op jit(solution)/shard_map/ppermute | solution.py:563
  9.2 7.5 %collective-permute-start = (f32[2,48,8,128]{3,2,1,0:T(8,128)S(1)}, f32[2,48,8,128]{3,2,1,0:T(8,128)S(1)}, u32[]{:S(2)}, u32[]{:S(2)}) collective-permute-start(f32[2,48,8,128]{3,2,1,0:T(8,128)S(1)} %get-tuple-element.27), channel_id=1, source_target_pairs={{0,4},{4,0},{1,5},{5,1},{2,6},{6,2},{3,7},{7,3},{8,12},{12,8},{9,1... | collective-permute-start | bytes 1179656 | tf_op jit(solution)/shard_map/ppermute | solution.py:565
  10.5 10.0 %collective-permute-start.2 = (f32[2,128,128]{2,1,0:T(8,128)S(1)}, f32[2,128,128]{2,1,0:T(8,128)S(1)}, u32[]{:S(2)}, u32[]{:S(2)}) collective-permute-start(f32[2,128,128]{2,1,0:T(8,128)S(1)} %get-tuple-element.29), channel_id=1, source_target_pairs={{8,16},{24,32},{40,48},{56,64},{72,80},{88,96},{104,112},{120,0},{... | collective-permute-start | bytes 393224 | tf_op jit(solution)/shard_map/ppermute | solution.py:567
  16.8 4.7 %collective-permute-start.1 = (f32[2,128,128]{2,1,0:T(8,128)S(1)}, f32[2,128,128]{2,1,0:T(8,128)S(1)}, u32[]{:S(2)}, u32[]{:S(2)}) collective-permute-start(f32[2,128,128]{2,1,0:T(8,128)S(1)} %get-tuple-element.29), channel_id=1, source_target_pairs={{0,8},{16,24},{32,40},{48,56},{64,72},{80,88},{96,104},{112,120},{... | collective-permute-start | bytes 393224 | tf_op jit(solution)/shard_map/ppermute | solution.py:566
  27.6 2.0 %collective-permute-start.5 = (f32[8,128]{1,0:T(8,128)S(1)}, f32[8,128]{1,0:T(8,128)S(1)}, u32[]{:S(2)}, u32[]{:S(2)}) collective-permute-start(f32[8,128]{1,0:T(8,128)S(1)} %get-tuple-element.37), channel_id=1, source_target_pairs={{0,4},{4,0},{1,5},{5,1},{2,6},{6,2},{3,7},{7,3},{8,12},{12,8},{9,1... | collective-permute-start | bytes 12296 | tf_op jit(solution)/shard_map/ppermute | solution.py:551
  48.3 2.6 %collective-permute-start.6 = (f32[8,128]{1,0:T(8,128)S(1)}, f32[8,128]{1,0:T(8,128)S(1)}, u32[]{:S(2)}, u32[]{:S(2)}) collective-permute-start(f32[8,128]{1,0:T(8,128)S(1)} %reduce_sum.9.mine_ref), channel_id=1, source_target_pairs={{0,4},{4,0},{1,5},{5,1},{2,6},{6,2},{3,7},{7,3},{8,12},{12,8},{9,1... | collective-permute-start | bytes 12296 | tf_op jit(solution)/shard_map/ppermute | solution.py:555

commit v4 on v3

--- a/solution.py
+++ b/solution.py
@@ -317,38 +317,37 @@
     return lax.broadcasted_iota(jnp.int32, (R, R), 0) % SUB == lax.broadcasted_iota(jnp.int32, (R, R), 1) % SUB
 
 
-def boundary_kernel(
-    v_ref, wy_ref, wx_ref, one_ref, two_ref, acc_ref, h_ref, l_ref, mine_ref, other_ref, sum_ref
-):
+def edge_level(which, v_ref, wy_ref, wx_ref, face_ref, acc_ref, h_ref, l_ref, sum_ref):
     vert = lax.axis_index("vert")
-    has_below, has_above = vert > 0, vert < lax.axis_size("vert") - 1
-
-    def vorticity(below_ref, above_ref):
-        def dz(c, s, k):
+
+    def vorticity(k):
+        inside = vert < lax.axis_size("vert") - 1 if k else vert > 0
+
+        def dz(c, s):
+            face = jnp.where(inside, face_ref[c, s], 0.0)
             if k:
-                return jnp.where(has_above, above_ref[c, s], 0.0) - v_ref[c, s, pl.ds((NZ - 2) * NY, NY), :]
-            return v_ref[c, s, pl.ds(NY, NY), :] - jnp.where(has_below, below_ref[c, s], 0.0)
-
-        for k in range(2):
-            for s in range(0, S, 2):
-                first = (0.5 * (wy_ref[k, t] - dz(1, t, k)) for t in (s, s + 1))
-                split_store(*first, s // 2, k, h_ref, l_ref)
-        for k in range(2):
-            for s in range(0, S, 2):
-                second = (0.5 * (dz(0, t, k) - wx_ref[k, t]) for t in (s, s + 1))
-                split_store(*second, s // 2, 2 + k, h_ref, l_ref)
-            if not k:
-                sum_ref[...] = acc_ref[...] + products(h_ref, l_ref, range(2))
-        sum_ref[...] += products(h_ref, l_ref, range(2, 4))
-
-    @pl.when(vert % 2 == 0)
-    def _():
-        vorticity(two_ref, one_ref)
-
-    @pl.when(vert % 2 == 1)
-    def _():
-        vorticity(one_ref, two_ref)
-
+                return face - v_ref[c, s, pl.ds((NZ - 2) * NY, NY), :]
+            return v_ref[c, s, pl.ds(NY, NY), :] - face
+
+        for s in range(0, S, 2):
+            first = (0.5 * (wy_ref[k, t] - dz(1, t)) for t in (s, s + 1))
+            split_store(*first, s // 2, 0, h_ref, l_ref)
+        for s in range(0, S, 2):
+            second = (0.5 * (dz(0, t) - wx_ref[k, t]) for t in (s, s + 1))
+            split_store(*second, s // 2, 1, h_ref, l_ref)
+        sum_ref[...] = acc_ref[...] + products(h_ref, l_ref, range(2))
+
+    @pl.when(vert % 2 == which)
+    def _():
+        vorticity(1)
+
+    @pl.when(vert % 2 == 1 - which)
+    def _():
+        vorticity(0)
+
+
+def last_edge_kernel(v_ref, wy_ref, wx_ref, face_ref, acc_ref, h_ref, l_ref, mine_ref, other_ref, sum_ref):
+    edge_level(1, v_ref, wy_ref, wx_ref, face_ref, acc_ref, h_ref, l_ref, sum_ref)
     total = sum_ref[...]
     total = jnp.where(same_cell(), total, 0.0).reshape(S, SUB, R).sum(1)
     total = lax.dot_general(
@@ -366,18 +365,19 @@
     other_ref[...] = jnp.where(first, bottom, top)
 
 
-def boundary(block, wy, wx, one, two, acc):
-    half = pltpu.VMEM((4, R, PAIR), BF16)
+def edge(which, block, wy, wx, face, acc):
+    half = pltpu.VMEM((2, R, PAIR), BF16)
     sums = pltpu.VMEM((SUB, NX), F32)
+    square = pltpu.VMEM((R, R), F32)
     return pl.pallas_call(
-        boundary_kernel,
-        name="boundary",
-        out_shape=(half, half, sums, sums),
-        in_specs=[vmem_spec()] * 6,
-        out_specs=(vmem_spec(),) * 4,
-        scratch_shapes=[pltpu.VMEM((R, R), F32)],
+        last_edge_kernel if which else functools.partial(edge_level, 0),
+        name="last_edge" if which else "first_edge",
+        out_shape=(half, half, sums, sums) if which else (half, half, square),
+        in_specs=[vmem_spec()] * 5,
+        out_specs=(vmem_spec(),) * (4 if which else 3),
+        scratch_shapes=[square] if which else [],
         compiler_params=params(8),
-    )(*in_vmem(block, wy, wx, one, two, acc))
+    )(*in_vmem(block, wy, wx, face, acc))
 
 
 def eliminate(work):
@@ -410,7 +410,8 @@
     return work
 
 
-def modes_kernel(count, mine_ref, other_ref, edge_h_ref, edge_l_ref, last_h_ref, last_l_ref, *refs):
+def modes_kernel(count, mine_ref, other_ref, *refs):
+    kept, refs = refs[:6], refs[6:]
     parts, (out_ref, factor_ref, h_ref, l_ref, wide_ref, corner_ref, buffer, sems, in_sems) = refs[:4], refs[4:]
     loads, start = [], 0
     for k in range(2):
@@ -471,16 +472,15 @@
     def copy_out(place):
         q = place - group
         if q < 0:
-            c, z = place // 2, place % 2 * (NZ - 1) if place < 4 else place + 2
+            odd = lax.axis_index("vert") % 2
+            c, z = (place % 2, (1 - odd, odd)[place // 2] * (NZ - 1)) if place < 4 else (2, place + 2)
         else:
             c, z = q // 6, q % 6 + (q < 12)
         return pltpu.make_async_copy(buffer.at[place], out_ref.at[c, :, z], sems.at[place])
 
     def source(place):
-        if place < 4:
-            return edge_h_ref[place], edge_l_ref[place]
         if place < group:
-            return last_h_ref[place - 4], last_l_ref[place - 4]
+            return tuple(ref[place % 2] for ref in kept[place // 2 * 2 : place // 2 * 2 + 2])
         return h_ref[place - group], l_ref[place - group]
 
     def apply(step):
@@ -526,7 +526,7 @@
             pltpu.HBM((3, S, NZ, NY, NX), F32),
             jax.ShapeDtypeStruct((S, S), F32),
         ),
-        in_specs=[vmem_spec()] * 6 + [any_spec()] * 4,
+        in_specs=[vmem_spec()] * 8 + [any_spec()] * 4,
         out_specs=(any_spec(), vmem_spec()),
         scratch_shapes=[pltpu.VMEM((18, R, PAIR), BF16)] * 2
         + [pltpu.VMEM((R, 6 * NX), BF16), pltpu.VMEM((2 * NX, 2 * NX), BF16)]
@@ -567,12 +567,13 @@
     odd = lax.ppermute(xs, "stream", neighbours("stream", 1))
     *head_halves, wy, wx, acc = first_component(v, hy)
     *rest_halves, wx, acc, last_high, last_low = other_components(v, hy, even, odd, wx, acc)
-    *edge_halves, mine, other = boundary(v, wy, wx, one, two, acc)
+    *near_halves, acc = edge(0, v, wy, wx, one, acc)
+    *far_halves, mine, other = edge(1, v, wy, wx, two, acc)
     mine, other = total_over_devices(mine, other)
     devices = lax.axis_size("stream") * lax.axis_size("span") * lax.axis_size("vert")
     count = float(3 * NZ * NY * NX * devices)
     return modes_and_factor(
-        mine, other, edge_halves + [last_high, last_low], head_halves + rest_halves, count
+        mine, other, near_halves + far_halves + [last_high, last_low], head_halves + rest_halves, count
     )
 
 

time: 59.8 us -> 59.2 us (0.990)
  blocking collectives: 18.6 us -> 17.8 us
    all_to_all x1, blocking collectives: 18.6 us -> 17.8 us  [total_over_devices(): lax.all_to_all(jnp.broadcast_to(mine, (peers,) + mine.shape), axes, 0, 0)]
    pallas_call x1 -> x2, Pallas kernels: 1.74 us -> 2.01 us  [edge(): pl.pallas_call(last_edge_kernel if which else functools.partial(edge_leve...]
  transfers between devices with their start and end apart: 7 -> 7, of which waited for: 4 -> 4; matrix products, arithmetic and copies ran while one was open for 0% -> 0% of each run, Pallas kernels for 17% -> 18%
where the time goes in v4:
time: 59.2 us; the launch traced here: 59 us
  Pallas kernels  22.1 us (37%)
  blocking collectives  17.8 us (30%)
  starting transfers between devices  14.3 us (24%)
  waiting for transfers between devices  3.79 us (6%)
  between operations  0.86 us (1%)
    all_to_all x1, blocking collectives, total_over_devices(): lax.all_to_all(jnp.broadcast_to(mine, (peers,) + mine.shape), axes, 0, 0)  17.8 us
    pallas_call x1, Pallas kernels, modes_and_factor(): pl.pallas_call(functools.partial(modes_kernel, count), name='modes', out_...  8.55 us
    ppermute x1, starting transfers between devices, per_device(): odd = lax.ppermute(xs, 'stream', neighbours('stream', 1))  6.22 us
    pallas_call x1, Pallas kernels, other_components(): pl.pallas_call(rest_kernel, name='other_components', out_shape=(half, hal...  4.39 us
    pallas_call x1, Pallas kernels, side_faces(): pl.pallas_call(side_faces_kernel, name='side_faces', out_shape=(pltpu.VME...  2.93 us
    pallas_call x1, Pallas kernels, first_component(): pl.pallas_call(first_kernel, name='first_component', out_shape=(half, hal...  2.57 us
    ppermute x1, starting transfers between devices, per_device(): one = lax.ppermute(one, 'vert', neighbours('vert', 0))  2.12 us
    pallas_call x2, Pallas kernels, edge(): pl.pallas_call(last_edge_kernel if which else functools.partial(edge_leve...  2.01 us
  transfers between devices with their start and end apart: 7, of which 4 were waited for; matrix products, arithmetic and copies ran while one was open for 0% of the time, Pallas kernels for 18%

profile of v4, /device:TPU:1, one launch (start us, length us, event | category | flops | bytes accessed | tf_op | source)
XLA Modules:
  0.0 59.0 jit_solution(9928605415674308277)
XLA Ops:
  0.6 0.0 copy-start
  0.6 1.7 %vertical_faces.1 = (f32[2,48,16,128]{3,2,1,0:T(8,128)S(1)}, f32[2,48,16,128]{3,2,1,0:T(8,128)S(1)}) custom-call(f32[3,48,128,128]{3,2,1,0:T(8,128)} %bitcast.2), custom_call_target="tpu_custom_call" | custom-call | tf_op jit(solution)/shard_map/vertical_faces/pallas_call | solution.py:62
  2.3 2.1 %collective-permute-start.4 = (f32[2,48,16,128]{3,2,1,0:T(8,128)S(1)}, f32[2,48,16,128]{3,2,1,0:T(8,128)S(1)}, u32[]{:S(2)}, u32[]{:S(2)}) collective-permute-start(f32[2,48,16,128]{3,2,1,0:T(8,128)S(1)} %get-tuple-element.37), channel_id=1, source_target_pairs={{0,1},{2,3},{1,0},{3,2},{4,5},{6,7},{5,4},{7,6},{8,9},{10,11},{9,8... | collective-permute-start | bytes 2359304 | tf_op jit(solution)/shard_map/ppermute | solution.py:562
  4.5 1.8 %collective-permute-start.3 = (f32[2,48,16,128]{3,2,1,0:T(8,128)S(1)}, f32[2,48,16,128]{3,2,1,0:T(8,128)S(1)}, u32[]{:S(2)}, u32[]{:S(2)}) collective-permute-start(f32[2,48,16,128]{3,2,1,0:T(8,128)S(1)} %get-tuple-element.36), channel_id=1, source_target_pairs={{1,2},{3,0},{2,1},{0,3},{5,6},{7,4},{6,5},{4,7},{9,10},{11,8},{10,... | collective-permute-start | bytes 2359304 | tf_op jit(solution)/shard_map/ppermute | solution.py:563
  6.3 0.0 copy-done
  6.3 2.9 %side_faces.1 = (f32[2,128,128]{2,1,0:T(8,128)S(1)}, f32[2,48,8,128]{3,2,1,0:T(8,128)S(1)}) custom-call(f32[3,48,128,128]{3,2,1,0:T(8,128)S(1)} %bitcast.3), custom_call_target="tpu_custom_call" | custom-call | tf_op jit(solution)/shard_map/side_faces/pallas_call | solution.py:96
  9.2 1.3 %collective-permute-start = (f32[2,48,8,128]{3,2,1,0:T(8,128)S(1)}, f32[2,48,8,128]{3,2,1,0:T(8,128)S(1)}, u32[]{:S(2)}, u32[]{:S(2)}) collective-permute-start(f32[2,48,8,128]{3,2,1,0:T(8,128)S(1)} %get-tuple-element.30), channel_id=1, source_target_pairs={{0,4},{4,0},{1,5},{5,1},{2,6},{6,2},{3,7},{7,3},{8,12},{12,8},{9,1... | collective-permute-start | bytes 1179656 | tf_op jit(solution)/shard_map/ppermute | solution.py:565
  10.5 6.2 %collective-permute-start.2 = (f32[2,128,128]{2,1,0:T(8,128)S(1)}, f32[2,128,128]{2,1,0:T(8,128)S(1)}, u32[]{:S(2)}, u32[]{:S(2)}) collective-permute-start(f32[2,128,128]{2,1,0:T(8,128)S(1)} %get-tuple-element.32), channel_id=1, source_target_pairs={{8,16},{24,32},{40,48},{56,64},{72,80},{88,96},{104,112},{120,0},{... | collective-permute-start | bytes 393224 | tf_op jit(solution)/shard_map/ppermute | solution.py:567
  16.8 0.0 collective-permute-start.1
  16.8 0.0 collective-permute-done.hy_ref
  16.8 2.6 %first_component.1 = (bf16[6,384,256]{2,1,0:T(8,128)(2,1)}, bf16[6,384,256]{2,1,0:T(8,128)(2,1)}, f32[2,48,16,128]{3,2,1,0:T(8,128)S(1)}, f32[6144,128]{1,0:T(8,128)S(1)}, f32[384,384]{1,0:T(8,128)S(1)}) custom-call(f32[3,6144,128]{2,1,0:T(8,128)S(1)} %bitcast.4, f32[2,48,8,128]{3,2,1,0:T(8,128)S(1)} %collective-permute-done.hy_ref), custom_call_target="tpu_custom_call" | custom-call | flops 905969664 | bytes 6291456 | tf_op jit(solution)/shard_map/first_component/pallas_call | solution.py:216
  19.3 1.2 %collective-permute-done.2.odd_ref = f32[2,128,128]{2,1,0:T(8,128)S(1)} collective-permute-done((f32[2,128,128]{2,1,0:T(8,128)S(1)}, f32[2,128,128]{2,1,0:T(8,128)S(1)}, u32[]{:S(2)}, u32[]{:S(2)}) %collective-permute-start.2) | collective-permute-done | bytes 131104 | tf_op jit(solution)/shard_map/ppermute | solution.py:567
  20.5 1.0 %collective-permute-done.1.even_ref = f32[2,128,128]{2,1,0:T(8,128)S(1)} collective-permute-done((f32[2,128,128]{2,1,0:T(8,128)S(1)}, f32[2,128,128]{2,1,0:T(8,128)S(1)}, u32[]{:S(2)}, u32[]{:S(2)}) %collective-permute-start.1) | collective-permute-done | bytes 131104 | tf_op jit(solution)/shard_map/ppermute | solution.py:566
  21.5 4.4 %other_components.1 = (bf16[12,384,256]{2,1,0:T(8,128)(2,1)}, bf16[12,384,256]{2,1,0:T(8,128)(2,1)}, f32[2,48,16,128]{3,2,1,0:T(8,128)S(1)}, f32[384,384]{1,0:T(...) custom-call(f32[3,6144,128]{2,1,0:T(8,128)S(1)} %bitcast.5, ...), custom_call_target="tpu_custom_call" | custom-call | flops 2113929216 | bytes 12582912 | tf_op jit(solution)/shard_map/other_components/pallas_call | solution.py:296
  25.9 0.0 collective-permute-done.4.face_ref
  25.9 0.7 %first_edge.1 = (bf16[2,384,256]{2,1,0:T(8,128)(2,1)S(1)}, bf16[2,384,256]{2,1,0:T(8,128)(2,1)S(1)}, f32[384,384]{1,0:T(8,128)S(1)}) custom-call(f32[3,48,128,128]{3,2,1,0:T(8,128)S(1)} %bitcast.6, f32[2,48,16,128]{3,2,1,0:T(8,128)S(1)} %get-tuple-element.31.wy_ref, f32[2,48,16,128]{3,2,1,0:T(8,128)S(1)} %get-tuple-element.35.wx_ref, ...), custom_call_target="tpu_custom_call" | custom-call | tf_op jit(solution)/shard_map/first_edge/pallas_call | solution.py:372
  26.6 0.0 collective-permute-done.3.face_ref
  26.6 1.3 %last_edge.1 = (bf16[2,384,256]{2,1,0:T(8,128)(2,1)S(1)}, bf16[2,384,256]{2,1,0:T(8,128)(2,1)S(1)}, f32[8,128]{1,0:T(8,128)S(1)}, f32[8,128]{1,0:T(8,128)S(1)}) custom-call(f32[3,48,128,128]{3,2,1,0:T(8,128)S(1)} %bitcast.7, f32[2,48,16,128]{3,2,1,0:T(8,128)S(1)} %get-tuple-element.31.wy_ref, f32[2,48,16,128]{3,2,1,0:T(8,128)S(1)} %get-tuple-element.35.wx_ref, ...), custom_call_target="tpu_custom_call" | custom-call | tf_op jit(solution)/shard_map/last_edge/pallas_call | solution.py:372
  27.9 1.2 %collective-permute-start.5 = (f32[8,128]{1,0:T(8,128)S(1)}, f32[8,128]{1,0:T(8,128)S(1)}, u32[]{:S(2)}, u32[]{:S(2)}) collective-permute-start(f32[8,128]{1,0:T(8,128)S(1)} %get-tuple-element.41), channel_id=1, source_target_pairs={{0,4},{4,0},{1,5},{5,1},{2,6},{6,2},{3,7},{7,3},{8,12},{12,8},{9,1... | collective-permute-start | bytes 12296 | tf_op jit(solution)/shard_map/ppermute | solution.py:551
  29.1 0.8 %collective-permute-done.5 = f32[8,128]{1,0:T(8,128)S(1)} collective-permute-done((f32[8,128]{1,0:T(8,128)S(1)}, f32[8,128]{1,0:T(8,128)S(1)}, u32[]{:S(2)}, u32[]{:S(2)}) %collective-permute-start.5) | collective-permute-done | bytes 4128 | tf_op jit(solution)/shard_map/ppermute | solution.py:551
  30.0 17.8 %all_to_all.5 = f32[64,8,128]{2,1,0:T(8,128)S(1)} all-to-all(f32[64,8,128]{2,1,0:T(8,128)S(1)} %broadcast_in_dim.3), channel_id=1, replica_groups=mesh['stream'=16,'span'=2,'vert'=4] {'stream','vert'}, dimensions={0} | all-to-all | bytes 524288 | tf_op jit(solution)/shard_map/all_to_all | solution.py:554
  47.8 0.1 reduce_sum.9.mine_ref
  47.9 1.6 %collective-permute-start.6 = (f32[8,128]{1,0:T(8,128)S(1)}, f32[8,128]{1,0:T(8,128)S(1)}, u32[]{:S(2)}, u32[]{:S(2)}) collective-permute-start(f32[8,128]{1,0:T(8,128)S(1)} %reduce_sum.9.mine_ref), channel_id=1, source_target_pairs={{0,4},{4,0},{1,5},{5,1},{2,6},{6,2},{3,7},{7,3},{8,12},{12,8},{9,1... | collective-permute-start | bytes 12296 | tf_op jit(solution)/shard_map/ppermute | solution.py:555
  49.5 0.8 %collective-permute-done.6.other_ref = f32[8,128]{1,0:T(8,128)S(1)} collective-permute-done((f32[8,128]{1,0:T(8,128)S(1)}, f32[8,128]{1,0:T(8,128)S(1)}, u32[]{:S(2)}, u32[]{:S(2)}) %collective-permute-start.6) | collective-permute-done | bytes 4128 | tf_op jit(solution)/shard_map/ppermute | solution.py:555
  50.3 8.5 %modes.1 = (f32[3,48,8,16,128]{4,3,2,1,0:T(8,128)}, f32[48,48]{1,0:T(8,128)}) custom-call(f32[8,128]{1,0:T(8,128)S(1)} %reduce_sum.9.mine_ref, f32[8,128]{1,0:T(8,128)S(1)} %collective-permute-done.6.other_ref, bf16[2,384,256]{2,1,0:T(8,128)(2,1)S(1)} %get-tuple-element.42.refs_0_, bf16[2,384,256]{2,1,0:T(8,128)(2,1)S(1)} %get-tuple-element.43.refs_1_, ...), custom_call_target="tpu_custom_call" | custom-call | tf_op jit(solution)/shard_map/modes/pallas_call | solution.py:522
  (2 shorter events, 0.0 us)
Async XLA Ops:
  0.6 5.6 %copy-start = (f32[3,48,8,16,128]{4,3,2,1,0:T(8,128)S(1)}, f32[3,48,8,16,128]{4,3,2,1,0:T(8,128)}, u32[]{:S(2)}) copy-start(f32[3,48,8,16,128]{4,3,2,1,0:T(8,128)} %param.1) | copy-start | bytes 28311556
  2.3 23.5 %collective-permute-start.4 = (f32[2,48,16,128]{3,2,1,0:T(8,128)S(1)}, f32[2,48,16,128]{3,2,1,0:T(8,128)S(1)}, u32[]{:S(2)}, u32[]{:S(2)}) collective-permute-start(f32[2,48,16,128]{3,2,1,0:T(8,128)S(1)} %get-tuple-element.37), channel_id=1, source_target_pairs={{0,1},{2,3},{1,0},{3,2},{4,5},{6,7},{5,4},{7,6},{8,9},{10,11},{9,8... | collective-permute-start | bytes 2359304 | tf_op jit(solution)/shard_map/ppermute | solution.py:562
  4.5 22.2 %collective-permute-start.3 = (f32[2,48,16,128]{3,2,1,0:T(8,128)S(1)}, f32[2,48,16,128]{3,2,1,0:T(8,128)S(1)}, u32[]{:S(2)}, u32[]{:S(2)}) collective-permute-start(f32[2,48,16,128]{3,2,1,0:T(8,128)S(1)} %get-tuple-element.36), channel_id=1, source_target_pairs={{1,2},{3,0},{2,1},{0,3},{5,6},{7,4},{6,5},{4,7},{9,10},{11,8},{10,... | collective-permute-start | bytes 2359304 | tf_op jit(solution)/shard_map/ppermute | solution.py:563
  9.2 7.5 %collective-permute-start = (f32[2,48,8,128]{3,2,1,0:T(8,128)S(1)}, f32[2,48,8,128]{3,2,1,0:T(8,128)S(1)}, u32[]{:S(2)}, u32[]{:S(2)}) collective-permute-start(f32[2,48,8,128]{3,2,1,0:T(8,128)S(1)} %get-tuple-element.30), channel_id=1, source_target_pairs={{0,4},{4,0},{1,5},{5,1},{2,6},{6,2},{3,7},{7,3},{8,12},{12,8},{9,1... | collective-permute-start | bytes 1179656 | tf_op jit(solution)/shard_map/ppermute | solution.py:565
  10.5 10.0 %collective-permute-start.2 = (f32[2,128,128]{2,1,0:T(8,128)S(1)}, f32[2,128,128]{2,1,0:T(8,128)S(1)}, u32[]{:S(2)}, u32[]{:S(2)}) collective-permute-start(f32[2,128,128]{2,1,0:T(8,128)S(1)} %get-tuple-element.32), channel_id=1, source_target_pairs={{8,16},{24,32},{40,48},{56,64},{72,80},{88,96},{104,112},{120,0},{... | collective-permute-start | bytes 393224 | tf_op jit(solution)/shard_map/ppermute | solution.py:567
  16.8 4.7 %collective-permute-start.1 = (f32[2,128,128]{2,1,0:T(8,128)S(1)}, f32[2,128,128]{2,1,0:T(8,128)S(1)}, u32[]{:S(2)}, u32[]{:S(2)}) collective-permute-start(f32[2,128,128]{2,1,0:T(8,128)S(1)} %get-tuple-element.32), channel_id=1, source_target_pairs={{0,8},{16,24},{32,40},{48,56},{64,72},{80,88},{96,104},{112,120},{... | collective-permute-start | bytes 393224 | tf_op jit(solution)/shard_map/ppermute | solution.py:566
  27.9 2.0 %collective-permute-start.5 = (f32[8,128]{1,0:T(8,128)S(1)}, f32[8,128]{1,0:T(8,128)S(1)}, u32[]{:S(2)}, u32[]{:S(2)}) collective-permute-start(f32[8,128]{1,0:T(8,128)S(1)} %get-tuple-element.41), channel_id=1, source_target_pairs={{0,4},{4,0},{1,5},{5,1},{2,6},{6,2},{3,7},{7,3},{8,12},{12,8},{9,1... | collective-permute-start | bytes 12296 | tf_op jit(solution)/shard_map/ppermute | solution.py:551
  47.9 2.4 %collective-permute-start.6 = (f32[8,128]{1,0:T(8,128)S(1)}, f32[8,128]{1,0:T(8,128)S(1)}, u32[]{:S(2)}, u32[]{:S(2)}) collective-permute-start(f32[8,128]{1,0:T(8,128)S(1)} %reduce_sum.9.mine_ref), channel_id=1, source_target_pairs={{0,4},{4,0},{1,5},{5,1},{2,6},{6,2},{3,7},{7,3},{8,12},{12,8},{9,1... | collective-permute-start | bytes 12296 | tf_op jit(solution)/shard_map/ppermute | solution.py:555
